TPU v7x, 1024 devices: a whole 4x8x16 slice. The times are simulated.
1024 devices in a mesh: dp: 32 (over z, core), node: 4 (over x), innode: 8 (over y).
Axes of the slice: x: 4, y: 8, z: 16, core: 2. Of those that a mesh axis runs over, the one named last changes fastest.
Arguments:
- tokens: bfloat16 [16384, 2048], P(('dp', 'node')), may hold values from -6 to 6
- routes: int32 [16384, 6], P(('dp', 'node')), may hold values from 0 to 31, as said below
- route_gates: float32 [16384, 6], P(('dp', 'node')), may hold values from 0.1 to 1
- out_grad: bfloat16 [16384, 2048], P(('dp', 'node')), may hold values from -4 to 4
- gate_weight: bfloat16 [32, 2048, 768], P(('node', 'innode'), 'dp'), may hold values from -0.125 to 0.125
- up_weight: bfloat16 [32, 2048, 768], P(('node', 'innode'), 'dp'), may hold values from -0.125 to 0.125
- down_weight: bfloat16 [32, 2048, 768], P(('node', 'innode'), 'dp'), may hold values from -0.21875 to 0.21875
Outputs:
- token_grad: bfloat16 [16384, 2048], P(('dp', 'node', 'innode'))
Inputs may be any that keep to these rules, and one draw needn't show every extreme that they name: `routes`: each row names 6 different experts, 3 in each of 2 different groups, the group of expert e being e // 8. In aligned blocks of 128 rows every group is named by the same number of rows, and no expert is named by more than 24 rows, a bound that some expert meets in every block.
All inputs are finite; a program needn't handle non-finite values.
Results may differ from a plain program's by a relative error of at most 0.015.
Values may be sent and summed in bfloat16 or wider, within the bound.
A program may use at most 64 MiB of HBM per device.

v0:
```python
import jax
import jax.numpy as jnp
from jax import lax
from jax.sharding import PartitionSpec as P


def local(tokens, routes, route_gates, out_grad, gate_weight, up_weight, down_weight):
    tok_count, width = tokens.shape
    top_count = routes.shape[1]
    groups = lax.axis_size("node")
    inner_size = lax.axis_size("innode")
    experts = groups * inner_size
    capacity = (top_count * tok_count + experts - 1) // experts
    inner_index = lax.axis_index("innode")
    flat_routes = routes.reshape(-1)
    matches = (flat_routes[:, None] == jnp.arange(experts, dtype=jnp.int32)[None, :]).astype(
        jnp.int32
    )
    earlier = jnp.cumsum(matches, axis=0) - matches
    slot_index = jnp.sum(earlier * matches, axis=1)
    position = jnp.where(
        flat_routes % inner_size == inner_index,
        flat_routes // inner_size * capacity + slot_index,
        -1,
    )
    owner = (position[:, None] == jnp.arange(groups * capacity, dtype=jnp.int32)[None, :]).astype(
        jnp.bfloat16
    )
    chosen = jnp.sum(
        owner.reshape(tok_count, top_count, groups * capacity).astype(jnp.float32), axis=1
    ).astype(jnp.bfloat16)
    contract_rows = (((0,), (0,)), ((), ()))
    sent_rows = lax.dot_general(
        chosen, tokens, contract_rows, preferred_element_type=jnp.float32
    ).astype(jnp.bfloat16)
    weighted = (out_grad.astype(jnp.float32)[:, None, :] * route_gates[:, :, None]).astype(
        jnp.bfloat16
    )
    sent_grad = lax.dot_general(
        owner,
        weighted.reshape(tok_count * top_count, width),
        contract_rows,
        preferred_element_type=jnp.float32,
    ).astype(jnp.bfloat16)
    got_rows, got_grad = (
        lax.all_to_all(
            sent_rows.reshape(groups, capacity, width),
            "node",
            split_axis=0,
            concat_axis=0,
            tiled=True,
        ),
        lax.all_to_all(
            sent_grad.reshape(groups, capacity, width),
            "node",
            split_axis=0,
            concat_axis=0,
            tiled=True,
        ),
    )
    rows_in = got_rows.reshape(groups * capacity, width)
    row_grad = got_grad.reshape(groups * capacity, width)
    gate_full, up_full, down_full = (
        lax.all_gather(gate_weight, "dp", axis=1, tiled=True),
        lax.all_gather(up_weight, "dp", axis=1, tiled=True),
        lax.all_gather(down_weight, "dp", axis=1, tiled=True),
    )
    hidden_grad = jnp.dot(row_grad, down_full[0], preferred_element_type=jnp.float32)
    gate_w = gate_full[0]
    up_w = up_full[0]
    gate_pre = jnp.dot(rows_in, gate_w, preferred_element_type=jnp.float32)
    up_pre = jnp.dot(rows_in, up_w, preferred_element_type=jnp.float32)
    sigma = jax.nn.sigmoid(gate_pre)
    gate_grad = (hidden_grad * up_pre * sigma * (1.0 + gate_pre * (1.0 - sigma))).astype(
        jnp.bfloat16
    )
    up_grad = (hidden_grad * gate_pre * sigma).astype(jnp.bfloat16)
    contract_width = (((1,), (1,)), ((), ()))
    back = (
        lax.dot_general(gate_grad, gate_w, contract_width, preferred_element_type=jnp.float32)
        + lax.dot_general(up_grad, up_w, contract_width, preferred_element_type=jnp.float32)
    ).astype(jnp.bfloat16)
    returned = lax.all_to_all(
        back.reshape(groups, capacity, width), "node", split_axis=0, concat_axis=0, tiled=True
    )
    partial_grad = jnp.dot(
        chosen, returned.reshape(groups * capacity, width), preferred_element_type=jnp.float32
    )
    summed = lax.psum(partial_grad.astype(jnp.bfloat16), "innode").astype(jnp.float32)
    share = tok_count // inner_size
    token_grad = lax.dynamic_slice_in_dim(summed, inner_index * share, share, 0).astype(
        jnp.bfloat16
    )
    return token_grad


def solution(mesh):
    return jax.shard_map(
        local,
        mesh=mesh,
        in_specs=(
            P(("dp", "node"), None),
            P(("dp", "node"), None),
            P(("dp", "node"), None),
            P(("dp", "node"), None),
            P(("node", "innode"), "dp", None),
            P(("node", "innode"), "dp", None),
            P(("node", "innode"), "dp", None),
        ),
        out_specs=P(("dp", "node", "innode"), None),
        check_vma=False,
    )
```

profile of v0, /device:TPU:1, one launch (start us, length us, event | category | flops | bytes accessed | tf_op | source)
XLA Modules:
  0.0 355.1 jit_solution(10767079356848202380)
XLA Ops:
  6.5 0.7 all-gather.4.cloned.1.call-update
  7.3 0.7 all-gather.8.cloned.1.call-update
  8.1 0.7 all-gather.6.cloned.1.call-update
  8.7 0.8 copy.17
  9.5 0.1 eq.64
  9.7 0.1 eq.68
  9.8 1.7 reduce-window.6
  11.6 0.3 slice_reduce_fusion
  11.9 5.3 %mul.62 = f32[128,6,2048]{2,1,0:T(8,128)} broadcast(bf16[128,2048]{1,0:T(8,128)(2,1)} %param.10), dimensions={0,2} | broadcast | bytes 6815744 | tf_op jit(solution)/shard_map/mul | solution.py:36
  17.2 8.3 %mul.63 = f32[768,2048]{1,0:T(8,128)} reshape(f32[128,6,2048]{2,1,0:T(8,128)} %mul.62) | data formatting | bytes 12582912 | tf_op jit(solution)/shard_map/mul | solution.py:36
  25.5 0.1 copy.25
  25.6 0.1 mul.64
  25.7 0.1 fusion.43
  25.8 4.3 %fusion.18 = bf16[96,2048]{1,0:T(8,128)(2,1)} fusion(f32[768,2048]{1,0:T(8,128)} %mul.63, f32[768]{0:T(1024)S(1)} %mul.64, s32[768]{0:T(1024)S(1)} %fusion.54), kind=kOutput, calls=%fused_computation.16 | convolution fusion | flops 305405952 | bytes 6690816 | tf_op jit(solution)/shard_map/dot_general | solution.py:39
  30.1 4.8 %all-to-all-start = ((bf16[4,24,2048]{2,1,0:T(8,128)(2,1)}), bf16[4,24,2048]{2,1,0:T(8,128)(2,1)S(1)}, u32[]{:S(2)}, u32[]{:S(2)}) async-start(bf16[4,24,2048]{2,1,0:T(8,128)(2,1)} %bitcast.1), calls=%async_computation | async-start | bytes 786432 | tf_op jit(solution)/shard_map/all_to_all | solution.py:53
  35.0 0.1 reduce_sum.24
  35.1 0.1 fusion.48
  35.2 0.1 copy.24
  35.3 1.0 convolution_convert_fusion.1
  36.3 4.9 %all-to-all-done = bf16[4,24,2048]{2,1,0:T(8,128)(2,1)S(1)} async-done(((bf16[4,24,2048]{2,1,0:T(8,128)(2,1)}), bf16[4,24,2048]{2,1,0:T(8,128)(2,1)S(1)}, u32[]{:S(2)}, u32[]{:S(2)}) %all-to-all-start) | async-done | bytes 393248 | tf_op jit(solution)/shard_map/all_to_all | solution.py:53
  41.2 3.5 all-to-all-start.1
  44.7 51.2 %all-gather.4.cloned.1.call-done = bf16[1,2048,768]{2,1,0:T(8,128)(2,1)} async-done(((bf16[1,64,768]{2,1,0:T(8,128)(2,1)}), bf16[1,2048,768]{2,1,0:T(8,128)(2,1)}) %all-gather.4.cloned.1.call-update) | async-done | bytes 3145744 | tf_op jit(solution)/shard_map/all_gather | solution.py:66
  95.9 2.5 fusion.9
  98.5 73.1 %all-gather.8.cloned.1.call-done = bf16[1,2048,768]{2,1,0:T(8,128)(2,1)} async-done(((bf16[1,64,768]{2,1,0:T(8,128)(2,1)}), bf16[1,2048,768]{2,1,0:T(8,128)(2,1)}) %all-gather.8.cloned.1.call-update) | async-done | bytes 3145744 | tf_op jit(solution)/shard_map/all_gather | solution.py:64
  171.6 2.5 fusion.3
  174.1 73.1 %all-gather.6.cloned.1.call-done = bf16[1,2048,768]{2,1,0:T(8,128)(2,1)} async-done(((bf16[1,64,768]{2,1,0:T(8,128)(2,1)}), bf16[1,2048,768]{2,1,0:T(8,128)(2,1)}) %all-gather.6.cloned.1.call-update) | async-done | bytes 3145744 | tf_op jit(solution)/shard_map/all_gather | solution.py:65
  247.2 4.5 %fusion.1 = f32[96,2048]{1,0:T(8,128)S(1)} fusion(bf16[1,2048,768]{2,1,0:T(8,128)(2,1)} %all-gather.8.cloned.1.call-done, f32[96,768]{1,0:T(8,128)S(1)} %fusion.9, bf16[96,2048]{1,0:T(8,128)(2,1)S(1)} %bitcast.61, bf16[1,2048,768]{2,1,0:T(8,128)(2,1)} %all-gather.6.cloned.1.call-done, f32[96,768]{1,0:T(8,128)S(1)} %fusion.3), kind=kOutput, calls=%fused_computation.2 | convolution fusion | flops 604717056 | bytes 8060928 | tf_op jit(solution)/shard_map/dot_general | solution.py:80
  251.7 3.0 fusion.15
  254.7 11.4 %all_to_all.15 = bf16[4,24,2048]{2,1,0:T(8,128)(2,1)S(1)} all-to-all(bf16[4,24,2048]{2,1,0:T(8,128)(2,1)S(1)} %bitcast.63), channel_id=1, replica_groups=mesh['dp'=32,'node'=4,'innode'=8] {'node'}, dimensions={0} | all-to-all | bytes 786432 | tf_op jit(solution)/shard_map/all_to_all | solution.py:83
  266.1 1.1 convolution_convert_fusion
  267.2 79.9 %all-reduce.2.cloned.1.call-done = bf16[128,2048]{1,0:T(8,128)(2,1)} async-done(((bf16[128,2048]{1,0:T(8,128)(2,1)}), bf16[128,2048]{1,0:T(8,128)(2,1)}) %all-reduce.2.cloned.1.call-update) | async-done | bytes 524304 | tf_op jit(solution)/shard_map/psum | solution.py:89
  347.1 1.5 convert_convert_fusion
  (14 shorter events, 0.3 us)
Async XLA Ops:
  6.5 28.8 %copy-start = (bf16[128,2048]{1,0:T(8,128)(2,1)S(1)}, bf16[128,2048]{1,0:T(8,128)(2,1)}, u32[]{:S(2)}) copy-start(bf16[128,2048]{1,0:T(8,128)(2,1)} %param.7) | copy-start | bytes 1572868
  6.5 89.4 %all-gather.4.cloned.1.call-start = ((), (), s32[]{:S(2)}) async-start(), calls=%async_computation.3 | async-start | bytes 3244032 | tf_op jit(solution)/shard_map/all_gather | solution.py:66
  7.3 164.3 %all-gather.8.cloned.1.call-start = ((), (), s32[]{:S(2)}) async-start(), calls=%async_computation.5 | async-start | bytes 3244032 | tf_op jit(solution)/shard_map/all_gather | solution.py:64
  8.0 239.1 %all-gather.6.cloned.1.call-start = ((), (), s32[]{:S(2)}) async-start(), calls=%async_computation.4 | async-start | bytes 3244032 | tf_op jit(solution)/shard_map/all_gather | solution.py:65
  17.2 8.3 %copy-start.1 = (f32[128,6]{0,1:T(8,128)S(1)}, f32[128,6]{0,1:T(8,128)}, u32[]{:S(2)}) copy-start(f32[128,6]{0,1:T(8,128)} %param.9) | copy-start | bytes 9220
  30.1 11.1 %all-to-all-start = ((bf16[4,24,2048]{2,1,0:T(8,128)(2,1)}), bf16[4,24,2048]{2,1,0:T(8,128)(2,1)S(1)}, u32[]{:S(2)}, u32[]{:S(2)}) async-start(bf16[4,24,2048]{2,1,0:T(8,128)(2,1)} %bitcast.1), calls=%async_computation | async-start | bytes 786432 | tf_op jit(solution)/shard_map/all_to_all | solution.py:53
  41.2 57.2 %all-to-all-start.1 = ((bf16[4,24,2048]{2,1,0:T(8,128)(2,1)}), bf16[4,24,2048]{2,1,0:T(8,128)(2,1)S(1)}, u32[]{:S(2)}, u32[]{:S(2)}) async-start(bf16[4,24,2048]{2,1,0:T(8,128)(2,1)} %bitcast.4), calls=%async_computation.1 | async-start | bytes 786432 | tf_op jit(solution)/shard_map/all_to_all | solution.py:46
  44.7 302.4 %all-reduce.2.cloned.1.call-start = ((), (), s32[]{:S(2)}) async-start(), calls=%async_computation.6 | async-start | bytes 1048576 | tf_op jit(solution)/shard_map/psum | solution.py:89
Sparse Core Ops, SparseCore 0:
  10.1 85.8 all-gather.3
  98.6 72.8 all-gather.7
  174.3 72.8 all-gather.5
  267.4 79.7 all-reduce.1
where the time goes:
time: 360 us; the launch traced here: 355 us
  waiting for transfers between devices  284 us (79%)
  matrix products  19 us (5%)
  local copies, waits for them, and re-layouts  15.3 us (4%)
  between operations  13.2 us (4%)
  blocking collectives  11.4 us (3%)
  starting transfers between devices  8.42 us (2%)
    psum x1, waiting for transfers between devices, local(): lax.psum(partial_grad.astype(jnp.bfloat16), 'innode').astype(jnp.float32)  79.9 us
    all_gather x1, waiting for transfers between devices, local(): lax.all_gather(gate_weight, 'dp', axis=1, tiled=True)  73.1 us
    all_gather x1, waiting for transfers between devices, local(): lax.all_gather(up_weight, 'dp', axis=1, tiled=True)  73.1 us
    all_gather x1, waiting for transfers between devices, local(): lax.all_gather(down_weight, 'dp', axis=1, tiled=True)  51.2 us
    mul x3, local copies, waits for them, and re-layouts, local(): out_grad.astype(jnp.float32)[:, None, :] * route_gates[:, :, None]  13.7 us
    all_to_all x1, blocking collectives, local(): lax.all_to_all(back.reshape(groups, capacity, width), 'node', split_axis=...  11.4 us
  transfers between devices with their start and end apart: 6, of which 5 were waited for; matrix products, arithmetic and copies ran while one was open for 8% of the time, Pallas kernels for 0%

commit v1 on v0

v1 whole, which is shorter than its diff:
```python
import functools

import jax
import jax.numpy as jnp
from jax import lax
from jax.experimental import pallas as pl
from jax.experimental.pallas import tpu as pltpu
from jax.sharding import PartitionSpec as P

MESH = pl.DeviceIdType.MESH
F32 = jnp.float32
BF16 = jnp.bfloat16

CW = 256
ROWS = 24
SLOT = 32
DC = 512


def body(
    nz, nx, ny,
    tok_hbm, routes_hbm, gates_hbm, grad_hbm, gate_hbm, up_hbm, down_hbm,
    out_ref,
    wbuf, tok, grd, rts, gts, xs, xr, lhs, acc, hid, back, ret_out, ret_in, part, yr,
    in_sem, own_sem, z_send, z_recv, p_send, p_recv, x_sem, r_send, r_recv, y_send, y_recv,
):
    half = nz // 2
    n_w = wbuf.shape[0]
    pairs = nz // 2
    n_dc = nz * 128 // DC
    dp = lax.axis_index("dp")
    x = lax.axis_index("node")
    y = lax.axis_index("innode")
    z, c = lax.div(dp, 2), lax.rem(dp, 2)
    nxt = lax.rem(z + 1, nz) * 2 + c
    prv = lax.rem(z + nz - 1, nz) * 2 + c
    ring = ({"dp": nxt}, {"dp": prv})
    partner = {"dp": z * 2 + 1 - c}
    x_to = [{"node": lax.rem(x + r, nx)} for r in range(nx)]
    x_back = [{"node": lax.rem(x + nx - r, nx)} for r in range(nx)]
    y_to = [{"innode": lax.rem(y + i, ny)} for i in range(ny)]

    def mine(ref, w, pos):
        return ref.at[w, :, pos, pl.ds(pl.multiple_of(c * 64, 64), 64), :]

    def mine2(w, s):
        return wbuf.at[w, :, pl.ds(2 * s, 2), pl.ds(pl.multiple_of(c * 64, 64), 64), :]

    def piece(w, pos, sub):
        return wbuf.at[w, :, pos, pl.ds(pl.multiple_of(c * 64 + sub * 32, 32), 32), :]

    own = []
    for w in range(n_w):
        for m, ref in enumerate((gate_hbm, up_hbm, down_hbm)):
            copy = pltpu.make_async_copy(
                ref.at[0, :, pl.ds(w * CW, CW)],
                wbuf.at[w, m, 0, pl.ds(pl.multiple_of(c * 64, 64), 64), :],
                own_sem.at[w, m],
            )
            copy.start()
            own.append(copy)
    ins = []
    for i, (a, b) in enumerate(
        ((routes_hbm, rts), (gates_hbm, gts), (tok_hbm, tok), (grad_hbm, grd))
    ):
        copy = pltpu.make_async_copy(a, b, in_sem.at[i])
        copy.start()
        ins.append(copy)

    barrier = pltpu.get_barrier_semaphore()
    peers = [ring[0], ring[1], partner] + x_to[1:] + y_to[1:]
    for peer in peers:
        pl.semaphore_signal(barrier, inc=1, device_id=peer, device_id_type=MESH)
    pl.semaphore_wait(barrier, len(peers))

    def z_copy(w, s, d, sub, src, dst):
        return pltpu.make_async_remote_copy(
            src_ref=piece(w, src, sub),
            dst_ref=piece(w, dst, sub),
            send_sem=z_send.at[w, s, d, sub],
            recv_sem=z_recv.at[w, s, d, sub],
            device_id=ring[d],
            device_id_type=MESH,
        )

    def p_copy(w, s):
        ref = mine2(w, s) if 0 < s < half else mine(wbuf, w, 0 if s == 0 else 1)
        return pltpu.make_async_remote_copy(
            src_ref=ref,
            dst_ref=ref,
            send_sem=p_send.at[w, s],
            recv_sem=p_recv.at[w, s],
            device_id=partner,
            device_id_type=MESH,
        )

    sent = []

    def start(copy):
        copy.start()
        sent.append(copy)

    def place(s, d):
        return 0 if s == 0 else (1 if s == half else 2 * s + d)

    def service(w, s):
        for sub in range(2):
            for d in range(2):
                if s == half and sub != d:
                    continue
                z_copy(w, s, d, sub, place(s - 1, d), place(s, d)).wait_recv()
                if s + 1 < half or (s + 1 == half and sub == d):
                    start(z_copy(w, s + 1, d, sub, place(s, d), place(s + 1, d)))
        start(p_copy(w, s))

    for w in range(n_w):
        for m in range(3):
            own[w * 3 + m].wait()
        for sub in range(2):
            for d in range(2):
                if half > 1 or sub == d:
                    start(z_copy(w, 1, d, sub, 0, place(1, d)))
    for w in range(n_w):
        start(p_copy(w, 0))

    ins[0].wait()
    ins[1].wait()
    n_tok = rts.shape[1]
    lanes = nx * SLOT
    line = lax.broadcasted_iota(jnp.int32, (lanes, n_tok), 0)
    slot = line & (SLOT - 1)
    group = x + (line >> 5)
    group = jnp.where(group >= nx, group - nx, group)
    expert = group * ny + y
    hit = jnp.zeros((lanes, n_tok), F32)
    weight = jnp.zeros((lanes, n_tok), F32)
    for k in range(rts.shape[0]):
        same = rts[k : k + 1, :] == expert
        hit = jnp.where(same, 1.0, hit)
        weight = jnp.where(same, gts[k : k + 1, :], weight)
    earlier = (
        lax.broadcasted_iota(jnp.int32, (n_tok, n_tok), 0)
        < lax.broadcasted_iota(jnp.int32, (n_tok, n_tok), 1)
    ).astype(F32).astype(BF16)
    rank = jnp.dot(hit.astype(BF16), earlier, preferred_element_type=F32)
    slot1 = jnp.where(slot < 16, slot, jnp.where(slot >= 24, slot - 8, -1))
    own0 = jnp.where(rank == slot.astype(F32), hit, 0.0)
    own1 = jnp.where(rank == slot1.astype(F32), hit, 0.0)
    pick = own0.astype(BF16)
    scale = jnp.sum(own0 * weight, axis=1, keepdims=True)
    spread = (jnp.transpose(own0).astype(BF16), jnp.transpose(own1).astype(BF16))

    ins[2].wait()
    ins[3].wait()
    for p in range(pairs):
        first = pl.multiple_of(lax.rem(z + nz - p, nz) * 128, 128)
        second = pl.multiple_of(lax.rem(z + (half if p == 0 else p), nz) * 128, 128)
        cols = pl.ds(p * 256, 256)
        a = jnp.concatenate([tok[:, pl.ds(first, 128)], tok[:, pl.ds(second, 128)]], axis=1)
        b = jnp.concatenate([grd[:, pl.ds(first, 128)], grd[:, pl.ds(second, 128)]], axis=1)
        a = jnp.dot(pick, a, preferred_element_type=F32)
        b = jnp.dot(pick, b, preferred_element_type=F32) * scale
        for r in range(nx):
            o = r * SLOT
            xs[r, 0:16, cols] = a[o : o + 16].astype(BF16)
            xs[r, 16:32, cols] = b[o : o + 16].astype(BF16)
            xs[r, 32:48, cols] = jnp.concatenate(
                [a[o + 16 : o + 24], b[o + 16 : o + 24]], axis=0
            ).astype(BF16)
    x_copies = []
    for r in range(1, nx):
        copy = pltpu.make_async_remote_copy(
            src_ref=xs.at[r],
            dst_ref=xr.at[r - 1],
            send_sem=x_sem.at[0, r],
            recv_sem=x_sem.at[1, r],
            device_id=x_to[r],
            device_id_type=MESH,
        )
        start(copy)
        x_copies.append(copy)

    def assemble():
        for copy in x_copies:
            copy.wait_recv()
        got = [xs.at[0]] + [xr.at[r - 1] for r in range(1, nx)]
        for r in range(nx):
            lhs[0, r * 16 : r * 16 + 16, :] = got[r][0:16, :]
            lhs[1, r * 16 : r * 16 + 16, :] = got[r][16:32, :]
        for r in range(0, nx, 2):
            a = got[r][32:48, :].astype(F32)
            b = got[r + 1][32:48, :].astype(F32)
            o = nx * 16 + r * 8
            lhs[0, o : o + 16, :] = jnp.concatenate([a[0:8], b[0:8]], axis=0).astype(BF16)
            lhs[1, o : o + 16, :] = jnp.concatenate([a[8:16], b[8:16]], axis=0).astype(BF16)

    def weights(w, m, p):
        return wbuf[w, m, 2 * p : 2 * p + 2].reshape(256, CW)

    def forward(w, p):
        cols = slice(p * 256, p * 256 + 256)
        if p == 0:
            p_copy(w, 0).wait_recv()
            p_copy(w, half).wait_recv()
        else:
            p_copy(w, p).wait_recv()
        for m in range(3):
            term = jnp.dot(
                lhs[m // 2, :, cols], weights(w, m, p), preferred_element_type=F32
            )
            if p == 1 or pairs == 1:
                acc[m] = term
            else:
                acc[m] += term

    def middle(w):
        gate_pre, up_pre, hidden = acc[0], acc[1], acc[2]
        sigma = 1.0 / (1.0 + jnp.exp(-gate_pre))
        hid[0] = (hidden * up_pre * sigma * (1.0 + gate_pre * (1.0 - sigma))).astype(BF16)
        hid[1] = (hidden * gate_pre * sigma).astype(BF16)

    over = (((1,), (1,)), ((), ()))

    def backward(w, p):
        cols = slice(p * 256, p * 256 + 256)
        term = lax.dot_general(hid[0], weights(w, 0, p), over, preferred_element_type=F32)
        term += lax.dot_general(hid[1], weights(w, 1, p), over, preferred_element_type=F32)
        if w == 0:
            back[:, cols] = term
        elif w + 1 < n_w:
            back[:, cols] += term
        else:
            return back[:, cols] + term

    steps = [(0, s) for s in range(1, half)]
    for w in range(n_w):
        if w + 1 < n_w:
            steps += [(w + 1, 1), (w, half)] if half > 1 else [(w, half), (w + 1, 1)]
            steps += [(w + 1, s) for s in range(2, half)]
        else:
            steps += [(w, half)]
    seen, steps2 = set(), []
    for step in steps:
        if step not in seen:
            seen.add(step)
            steps2.append(step)
    order = list(range(1, pairs)) + [0]
    queue = [(0, None, assemble)]
    for w in range(n_w):
        for p in order:
            queue.append((3, (w, p if p else half), functools.partial(forward, w, p)))
        queue.append((2, None, functools.partial(middle, w)))
        if w + 1 < n_w:
            for p in order:
                queue.append((2, None, functools.partial(backward, w, p)))
    done = set()
    for i, step in enumerate(steps2):
        service(*step)
        if i >= min(5, half - 1):
            budget = 10
            while queue and budget > 0 and (queue[0][1] is None or queue[0][1] in done):
                cost, _, work = queue.pop(0)
                work()
                budget -= cost
        done.add(step)
    for _, _, work in queue:
        work()

    last = n_w - 1
    ret = []
    for dc in range(n_dc):
        a, b = backward(last, 2 * dc), backward(last, 2 * dc + 1)
        for r in range(nx):
            o, q = r * 16, nx * 16 + r * 8
            dest = ret_in.at[dc, 0] if r == 0 else ret_out.at[dc, r - 1]
            dest[0:16, :] = a[o : o + 16].astype(BF16)
            dest[16:32, :] = b[o : o + 16].astype(BF16)
            dest[32:48, :] = jnp.concatenate([a[q : q + 8], b[q : q + 8]], axis=0).astype(BF16)
        ret.append([])
        for r in range(1, nx):
            copy = pltpu.make_async_remote_copy(
                src_ref=ret_out.at[dc, r - 1],
                dst_ref=ret_in.at[dc, r],
                send_sem=r_send.at[dc, r],
                recv_sem=r_recv.at[dc, r],
                device_id=x_back[r],
                device_id_type=MESH,
            )
            start(copy)
            ret[-1].append(copy)
    y_copies = []
    for dc in range(n_dc):
        for copy in ret[dc]:
            copy.wait_recv()
        for h in range(2):
            rows = []
            for r in range(nx):
                rows += [ret_in[dc, r, h * 16 : h * 16 + 16, :], ret_in[dc, r, 32:48, :]]
            part[dc, :, h * 256 : h * 256 + 256] = jnp.dot(
                spread[h], jnp.concatenate(rows, axis=0), preferred_element_type=F32
            ).astype(BF16)
        y_copies.append([])
        for i in range(1, ny):
            to = pl.multiple_of(lax.rem(y + i, ny) * 16, 16)
            copy = pltpu.make_async_remote_copy(
                src_ref=part.at[dc, pl.ds(to, 16), :],
                dst_ref=yr.at[dc, i - 1],
                send_sem=y_send.at[dc, i],
                recv_sem=y_recv.at[dc, i],
                device_id=y_to[i],
                device_id_type=MESH,
            )
            start(copy)
            y_copies[-1].append(copy)
    for dc in range(n_dc):
        total = part[dc, pl.ds(pl.multiple_of(y * 16, 16), 16), :].astype(F32)
        for i in range(1, ny):
            y_copies[dc][i - 1].wait_recv()
            total += yr[dc, i - 1].astype(F32)
        total = total.astype(BF16)
        for i in range(DC // 128):
            pos = dc * (DC // 128) + i
            p = pos // 2
            if pos % 2 == 0:
                src = lax.rem(z + nz - p, nz)
            else:
                src = lax.rem(z + (half if p == 0 else p), nz)
            out_ref[:, pl.ds(pl.multiple_of(src * 128, 128), 128)] = total[
                :, i * 128 : i * 128 + 128
            ]
    for copy in sent:
        copy.wait_send()


def solution(mesh):
    nz, nx, ny = mesh.shape["dp"] // 2, mesh.shape["node"], mesh.shape["innode"]

    def local(tokens, routes, route_gates, out_grad, gate_weight, up_weight, down_weight):
        n_tok, width = tokens.shape
        n_w = gate_weight.shape[2] // CW
        rows = nx * ROWS
        n_dc = width // DC
        half = nz // 2
        any_space = pl.BlockSpec(memory_space=pl.ANY)
        dma = pltpu.SemaphoreType.DMA
        return pl.pallas_call(
            functools.partial(body, nz, nx, ny),
            out_shape=jax.ShapeDtypeStruct((n_tok // ny, width), BF16),
            in_specs=[any_space] * 7,
            out_specs=pl.BlockSpec(memory_space=pltpu.VMEM),
            scratch_shapes=[
                pltpu.VMEM((n_w, 3, nz, 128, CW), BF16),
                pltpu.VMEM((n_tok, width), BF16),
                pltpu.VMEM((n_tok, width), BF16),
                pltpu.VMEM(routes.shape[::-1], jnp.int32),
                pltpu.VMEM(route_gates.shape[::-1], F32),
                pltpu.VMEM((nx, 48, width), BF16),
                pltpu.VMEM((nx - 1, 48, width), BF16),
                pltpu.VMEM((2, rows, width), BF16),
                pltpu.VMEM((3, rows, CW), F32),
                pltpu.VMEM((2, rows, CW), BF16),
                pltpu.VMEM((rows, width), F32),
                pltpu.VMEM((n_dc, nx - 1, 48, 256), BF16),
                pltpu.VMEM((n_dc, nx, 48, 256), BF16),
                pltpu.VMEM((n_dc, n_tok, DC), BF16),
                pltpu.VMEM((n_dc, max(ny - 1, 1), n_tok // ny, DC), BF16),
                dma((4,)),
                dma((n_w, 3)),
                dma((n_w, half + 1, 2, 2)),
                dma((n_w, half + 1, 2, 2)),
                dma((n_w, half + 1)),
                dma((n_w, half + 1)),
                dma((2, nx)),
                dma((n_dc, nx)),
                dma((n_dc, nx)),
                dma((n_dc, ny)),
                dma((n_dc, ny)),
            ],
            compiler_params=pltpu.CompilerParams(
                collective_id=0, has_side_effects=True, vmem_limit_bytes=60 * 1024 * 1024
            ),
            cost_estimate=pl.CostEstimate(
                flops=10 * rows * width * gate_weight.shape[2],
                bytes_accessed=16 * 1024 * 1024,
                transcendentals=rows * gate_weight.shape[2],
            ),
            name="moe_input_grad",
        )(tokens, routes.T, route_gates.T, out_grad, gate_weight, up_weight, down_weight)

    return jax.shard_map(
        local,
        mesh=mesh,
        in_specs=(
            P(("dp", "node"), None),
            P(("dp", "node"), None),
            P(("dp", "node"), None),
            P(("dp", "node"), None),
            P(("node", "innode"), "dp", None),
            P(("node", "innode"), "dp", None),
            P(("node", "innode"), "dp", None),
        ),
        out_specs=P(("dp", "node", "innode"), None),
        check_vma=False,
    )
```

time: 360 us -> 123 us (0.34); the launches traced: 355 us -> 123 us
  waiting for transfers between devices: 284 us -> 0 us
  Pallas kernels: 0 us -> 122 us
  matrix products: 19 us -> 0 us
  local copies, waits for them, and re-layouts: 15.3 us -> 1.47 us
  between operations: 13.2 us -> 0.01 us
  blocking collectives: 11.4 us -> 0 us
  starting transfers between devices: 8.42 us -> 0 us
    all_gather x3 -> x0, waiting for transfers between devices: 197 us -> none  [the longest x1 73.1 us: local(): lax.all_gather(gate_weight, 'dp', axis=1, tiled=True)]
    pallas_call x0 -> x1, Pallas kernels: none -> 122 us  [local(): pl.pallas_call(functools.partial(body, nz, nx, ny), out_shape=jax.ShapeDt...]
    psum x1 -> x0, waiting for transfers between devices: 79.9 us -> none  [local(): lax.psum(partial_grad.astype(jnp.bfloat16), 'innode').astype(jnp.float32)]
    dot_general x7 -> x0, matrix products: 19 us -> none  [the longest x1 4.55 us: local(): lax.dot_general(gate_grad, gate_w, contract_width, preferred_element_type...]
    mul x3 -> x0, local copies, waits for them, and re-layouts: 13.7 us -> none  [local(): out_grad.astype(jnp.float32)[:, None, :] * route_gates[:, :, None]]
    all_to_all x1 -> x0, blocking collectives: 11.4 us -> none  [local(): lax.all_to_all(back.reshape(groups, capacity, width), 'node', split_axis=...]
    all_to_all x2 -> x0, starting transfers between devices: 8.3 us -> none  [the longest x1 4.84 us: local(): lax.all_to_all(sent_grad.reshape(groups, capacity, width), 'node', split_...]
    all_to_all x2 -> x0, waiting for transfers between devices: 4.88 us -> none  [the longest x1 4.88 us: local(): lax.all_to_all(sent_grad.reshape(groups, capacity, width), 'node', split_...]
  transfers between devices with their start and end apart: 6 -> 0, of which waited for: 5 -> 0; matrix products, arithmetic and copies ran while one was open for 8% -> 0% of each run, Pallas kernels for 0% -> 0%
where the time goes in v1:
time: 123 us
  Pallas kernels  122 us (99%)
  local copies, waits for them, and re-layouts  1.47 us (1%)
    pallas_call x1, Pallas kernels, local(): pl.pallas_call(functools.partial(body, nz, nx, ny), out_shape=jax.ShapeDt...  122 us

profile of v1, /device:TPU:1, one launch (start us, length us, event | category | flops | bytes accessed | tf_op | source)
XLA Modules:
  0.0 123.1 jit_solution(2515444509353174031)
XLA Ops:
  0.0 121.6 %moe_input_grad.1 = bf16[16,2048]{1,0:T(8,128)(2,1)} custom-call(bf16[128,2048]{1,0:T(8,128)(2,1)} %tok_hbm.1, s32[6,128]{1,0:T(8,128)} %bitcast.2, f32[6,128]{1,0:T(8,128)} %bitcast.3, bf16[128,2048]{1,0:T(8,128)(2,1)} %grad_hbm.1, bf16[1,64,768]{2,1,0:T(8,128)(2,1)} %gate_hbm.1, bf16[1,64,768]{2,1,0:T(8,128)(2,1)} %up_hbm.1, bf16[1,64,768]{2,1,0:T(8,128)(2,1)} %down_hbm.1), custom_call_target="tpu_custom_call" | custom-call | flops 1509949440 | bytes 16777216 | tf_op jit(solution)/shard_map/moe_input_grad/pallas_call | solution.py:346
  121.6 1.5 %copy.9 = bf16[16,2048]{1,0:T(8,128)(2,1)} copy(bf16[16,2048]{1,0:T(8,128)(2,1)} %moe_input_grad.1) | data formatting | bytes 131072

commit v2 on v1

--- a/solution.py
+++ b/solution.py
@@ -11,7 +11,6 @@
 F32 = jnp.float32
 BF16 = jnp.bfloat16
 
-CW = 256
 ROWS = 24
 SLOT = 32
 DC = 512
@@ -21,11 +20,10 @@
     nz, nx, ny,
     tok_hbm, routes_hbm, gates_hbm, grad_hbm, gate_hbm, up_hbm, down_hbm,
     out_ref,
-    wbuf, tok, grd, rts, gts, xs, xr, lhs, acc, hid, back, ret_out, ret_in, part, yr,
+    wbuf, tok, grd, rts, gts, xs, xr, lhs, acc, hid, ret_out, ret_in, part, yr,
     in_sem, own_sem, z_send, z_recv, p_send, p_recv, x_sem, r_send, r_recv, y_send, y_recv,
 ):
     half = nz // 2
-    n_w = wbuf.shape[0]
     pairs = nz // 2
     n_dc = nz * 128 // DC
     dp = lax.axis_index("dp")
@@ -40,25 +38,19 @@
     x_back = [{"node": lax.rem(x + nx - r, nx)} for r in range(nx)]
     y_to = [{"innode": lax.rem(y + i, ny)} for i in range(ny)]
 
-    def mine(ref, w, pos):
-        return ref.at[w, :, pos, pl.ds(pl.multiple_of(c * 64, 64), 64), :]
-
-    def mine2(w, s):
-        return wbuf.at[w, :, pl.ds(2 * s, 2), pl.ds(pl.multiple_of(c * 64, 64), 64), :]
-
-    def piece(w, pos, sub):
-        return wbuf.at[w, :, pos, pl.ds(pl.multiple_of(c * 64 + sub * 32, 32), 32), :]
+    def mine(m, pos, count):
+        return wbuf.at[m, pl.ds(pos, count), pl.ds(pl.multiple_of(c * 64, 64), 64), :]
+
+    def piece(m, pos, s, d):
+        if s == half:
+            return wbuf.at[m, pos, pl.ds(pl.multiple_of(c * 64 + d * 32, 32), 32), :]
+        return wbuf.at[m, pos, pl.ds(pl.multiple_of(c * 64, 64), 64), :]
 
     own = []
-    for w in range(n_w):
-        for m, ref in enumerate((gate_hbm, up_hbm, down_hbm)):
-            copy = pltpu.make_async_copy(
-                ref.at[0, :, pl.ds(w * CW, CW)],
-                wbuf.at[w, m, 0, pl.ds(pl.multiple_of(c * 64, 64), 64), :],
-                own_sem.at[w, m],
-            )
-            copy.start()
-            own.append(copy)
+    for m, ref in enumerate((gate_hbm, up_hbm, down_hbm)):
+        copy = pltpu.make_async_copy(ref, mine(m, 0, 1), own_sem.at[m])
+        copy.start()
+        own.append(copy)
     ins = []
     for i, (a, b) in enumerate(
         ((routes_hbm, rts), (gates_hbm, gts), (tok_hbm, tok), (grad_hbm, grd))
@@ -73,23 +65,23 @@
         pl.semaphore_signal(barrier, inc=1, device_id=peer, device_id_type=MESH)
     pl.semaphore_wait(barrier, len(peers))
 
-    def z_copy(w, s, d, sub, src, dst):
+    def z_copy(s, m, d):
         return pltpu.make_async_remote_copy(
-            src_ref=piece(w, src, sub),
-            dst_ref=piece(w, dst, sub),
-            send_sem=z_send.at[w, s, d, sub],
-            recv_sem=z_recv.at[w, s, d, sub],
+            src_ref=piece(m, place(s - 1, d), s, d),
+            dst_ref=piece(m, place(s, d), s, d),
+            send_sem=z_send.at[s, m, d],
+            recv_sem=z_recv.at[s, m, d],
             device_id=ring[d],
             device_id_type=MESH,
         )
 
-    def p_copy(w, s):
-        ref = mine2(w, s) if 0 < s < half else mine(wbuf, w, 0 if s == 0 else 1)
+    def p_copy(s, m):
+        ref = mine(m, 2 * s, 2) if 0 < s < half else mine(m, 0 if s == 0 else 1, 1)
         return pltpu.make_async_remote_copy(
             src_ref=ref,
             dst_ref=ref,
-            send_sem=p_send.at[w, s],
-            recv_sem=p_recv.at[w, s],
+            send_sem=p_send.at[s, m],
+            recv_sem=p_recv.at[s, m],
             device_id=partner,
             device_id_type=MESH,
         )
@@ -103,25 +95,20 @@
     def place(s, d):
         return 0 if s == 0 else (1 if s == half else 2 * s + d)
 
-    def service(w, s):
-        for sub in range(2):
+    def service(s):
+        for m in range(3):
             for d in range(2):
-                if s == half and sub != d:
-                    continue
-                z_copy(w, s, d, sub, place(s - 1, d), place(s, d)).wait_recv()
-                if s + 1 < half or (s + 1 == half and sub == d):
-                    start(z_copy(w, s + 1, d, sub, place(s, d), place(s + 1, d)))
-        start(p_copy(w, s))
-
-    for w in range(n_w):
-        for m in range(3):
-            own[w * 3 + m].wait()
-        for sub in range(2):
-            for d in range(2):
-                if half > 1 or sub == d:
-                    start(z_copy(w, 1, d, sub, 0, place(1, d)))
-    for w in range(n_w):
-        start(p_copy(w, 0))
+                z_copy(s, m, d).wait_recv()
+                if s < half:
+                    start(z_copy(s + 1, m, d))
+            start(p_copy(s, m))
+
+    for m in range(3):
+        own[m].wait()
+        for d in range(2):
+            start(z_copy(1, m, d))
+    for m in range(3):
+        start(p_copy(0, m))
 
     ins[0].wait()
     ins[1].wait()
@@ -194,82 +181,59 @@
             lhs[0, o : o + 16, :] = jnp.concatenate([a[0:8], b[0:8]], axis=0).astype(BF16)
             lhs[1, o : o + 16, :] = jnp.concatenate([a[8:16], b[8:16]], axis=0).astype(BF16)
 
-    def weights(w, m, p):
-        return wbuf[w, m, 2 * p : 2 * p + 2].reshape(256, CW)
-
-    def forward(w, p):
-        cols = slice(p * 256, p * 256 + 256)
+    def forward(p, m):
         if p == 0:
-            p_copy(w, 0).wait_recv()
-            p_copy(w, half).wait_recv()
+            p_copy(0, m).wait_recv()
+            p_copy(half, m).wait_recv()
         else:
-            p_copy(w, p).wait_recv()
+            p_copy(p, m).wait_recv()
+        width = wbuf.shape[3]
+        term = jnp.dot(
+            lhs[m // 2, :, p * 256 : p * 256 + 256],
+            wbuf[m, 2 * p : 2 * p + 2].reshape(256, width),
+            preferred_element_type=F32,
+        )
+        if p == (1 if pairs > 1 else 0):
+            acc[m] = term
+        else:
+            acc[m] += term
+
+    wait_steps = min(3, half - 1)
+    ready = []
+    for s in range(1, half):
+        service(s)
+        if s == wait_steps:
+            assemble()
+        if s >= wait_steps:
+            while ready:
+                p = ready.pop(0)
+                for m in range(3):
+                    forward(p, m)
+        ready.append(s)
+    for p in ready:
         for m in range(3):
-            term = jnp.dot(
-                lhs[m // 2, :, cols], weights(w, m, p), preferred_element_type=F32
-            )
-            if p == 1 or pairs == 1:
-                acc[m] = term
-            else:
-                acc[m] += term
-
-    def middle(w):
-        gate_pre, up_pre, hidden = acc[0], acc[1], acc[2]
-        sigma = 1.0 / (1.0 + jnp.exp(-gate_pre))
-        hid[0] = (hidden * up_pre * sigma * (1.0 + gate_pre * (1.0 - sigma))).astype(BF16)
-        hid[1] = (hidden * gate_pre * sigma).astype(BF16)
+            forward(p, m)
+    service(half)
+    for m in range(3):
+        forward(0, m)
+    gate_pre, up_pre, hidden = acc[0], acc[1], acc[2]
+    sigma = 1.0 / (1.0 + jnp.exp(-gate_pre))
+    hid[0] = (hidden * up_pre * sigma * (1.0 + gate_pre * (1.0 - sigma))).astype(BF16)
+    hid[1] = (hidden * gate_pre * sigma).astype(BF16)
 
     over = (((1,), (1,)), ((), ()))
 
-    def backward(w, p):
-        cols = slice(p * 256, p * 256 + 256)
-        term = lax.dot_general(hid[0], weights(w, 0, p), over, preferred_element_type=F32)
-        term += lax.dot_general(hid[1], weights(w, 1, p), over, preferred_element_type=F32)
-        if w == 0:
-            back[:, cols] = term
-        elif w + 1 < n_w:
-            back[:, cols] += term
-        else:
-            return back[:, cols] + term
-
-    steps = [(0, s) for s in range(1, half)]
-    for w in range(n_w):
-        if w + 1 < n_w:
-            steps += [(w + 1, 1), (w, half)] if half > 1 else [(w, half), (w + 1, 1)]
-            steps += [(w + 1, s) for s in range(2, half)]
-        else:
-            steps += [(w, half)]
-    seen, steps2 = set(), []
-    for step in steps:
-        if step not in seen:
-            seen.add(step)
-            steps2.append(step)
-    order = list(range(1, pairs)) + [0]
-    queue = [(0, None, assemble)]
-    for w in range(n_w):
-        for p in order:
-            queue.append((3, (w, p if p else half), functools.partial(forward, w, p)))
-        queue.append((2, None, functools.partial(middle, w)))
-        if w + 1 < n_w:
-            for p in order:
-                queue.append((2, None, functools.partial(backward, w, p)))
-    done = set()
-    for i, step in enumerate(steps2):
-        service(*step)
-        if i >= min(5, half - 1):
-            budget = 10
-            while queue and budget > 0 and (queue[0][1] is None or queue[0][1] in done):
-                cost, _, work = queue.pop(0)
-                work()
-                budget -= cost
-        done.add(step)
-    for _, _, work in queue:
-        work()
-
-    last = n_w - 1
+    def backward(p):
+        term = None
+        for m in range(2):
+            rhs = wbuf[m, 2 * p : 2 * p + 2].reshape(256, wbuf.shape[3])
+            part_sum = lax.dot_general(hid[m], rhs, over, preferred_element_type=F32)
+            term = part_sum if term is None else term + part_sum
+        return term
+
     ret = []
     for dc in range(n_dc):
-        a, b = backward(last, 2 * dc), backward(last, 2 * dc + 1)
+        a, b = backward(2 * dc), backward(2 * dc + 1)
         for r in range(nx):
             o, q = r * 16, nx * 16 + r * 8
             dest = ret_in.at[dc, 0] if r == 0 else ret_out.at[dc, r - 1]
@@ -337,7 +301,7 @@
 
     def local(tokens, routes, route_gates, out_grad, gate_weight, up_weight, down_weight):
         n_tok, width = tokens.shape
-        n_w = gate_weight.shape[2] // CW
+        units = gate_weight.shape[2]
         rows = nx * ROWS
         n_dc = width // DC
         half = nz // 2
@@ -349,7 +313,7 @@
             in_specs=[any_space] * 7,
             out_specs=pl.BlockSpec(memory_space=pltpu.VMEM),
             scratch_shapes=[
-                pltpu.VMEM((n_w, 3, nz, 128, CW), BF16),
+                pltpu.VMEM((3, nz, 128, units), BF16),
                 pltpu.VMEM((n_tok, width), BF16),
                 pltpu.VMEM((n_tok, width), BF16),
                 pltpu.VMEM(routes.shape[::-1], jnp.int32),
@@ -357,19 +321,18 @@
                 pltpu.VMEM((nx, 48, width), BF16),
                 pltpu.VMEM((nx - 1, 48, width), BF16),
                 pltpu.VMEM((2, rows, width), BF16),
-                pltpu.VMEM((3, rows, CW), F32),
-                pltpu.VMEM((2, rows, CW), BF16),
-                pltpu.VMEM((rows, width), F32),
+                pltpu.VMEM((3, rows, units), F32),
+                pltpu.VMEM((2, rows, units), BF16),
                 pltpu.VMEM((n_dc, nx - 1, 48, 256), BF16),
                 pltpu.VMEM((n_dc, nx, 48, 256), BF16),
                 pltpu.VMEM((n_dc, n_tok, DC), BF16),
                 pltpu.VMEM((n_dc, max(ny - 1, 1), n_tok // ny, DC), BF16),
                 dma((4,)),
-                dma((n_w, 3)),
-                dma((n_w, half + 1, 2, 2)),
-                dma((n_w, half + 1, 2, 2)),
-                dma((n_w, half + 1)),
-                dma((n_w, half + 1)),
+                dma((3,)),
+                dma((half + 1, 3, 2)),
+                dma((half + 1, 3, 2)),
+                dma((half + 1, 3)),
+                dma((half + 1, 3)),
                 dma((2, nx)),
                 dma((n_dc, nx)),
                 dma((n_dc, nx)),
@@ -380,9 +343,9 @@
                 collective_id=0, has_side_effects=True, vmem_limit_bytes=60 * 1024 * 1024
             ),
             cost_estimate=pl.CostEstimate(
-                flops=10 * rows * width * gate_weight.shape[2],
+                flops=10 * rows * width * units,
                 bytes_accessed=16 * 1024 * 1024,
-                transcendentals=rows * gate_weight.shape[2],
+                transcendentals=rows * units,
             ),
             name="moe_input_grad",
         )(tokens, routes.T, route_gates.T, out_grad, gate_weight, up_weight, down_weight)

time: 123 us -> 97.2 us (0.79)
  Pallas kernels: 122 us -> 95.6 us
    pallas_call x1, Pallas kernels: 122 us -> 95.6 us  [local(): pl.pallas_call(functools.partial(body, nz, nx, ny), out_shape=jax.ShapeDt...]
where the time goes in v2:
time: 97.2 us; the launch traced here: 97.1 us
  Pallas kernels  95.6 us (98%)
  local copies, waits for them, and re-layouts  1.47 us (2%)
    pallas_call x1, Pallas kernels, local(): pl.pallas_call(functools.partial(body, nz, nx, ny), out_shape=jax.ShapeDt...  95.6 us

profile of v2, /device:TPU:1, one launch (start us, length us, event | category | flops | bytes accessed | tf_op | source)
XLA Modules:
  0.0 97.1 jit_solution(17318146456352018287)
XLA Ops:
  0.0 95.6 %moe_input_grad.1 = bf16[16,2048]{1,0:T(8,128)(2,1)} custom-call(bf16[128,2048]{1,0:T(8,128)(2,1)} %tok_hbm.1, s32[6,128]{1,0:T(8,128)} %bitcast.2, f32[6,128]{1,0:T(8,128)} %bitcast.3, bf16[128,2048]{1,0:T(8,128)(2,1)} %grad_hbm.1, bf16[1,64,768]{2,1,0:T(8,128)(2,1)} %gate_hbm.1, bf16[1,64,768]{2,1,0:T(8,128)(2,1)} %up_hbm.1, bf16[1,64,768]{2,1,0:T(8,128)(2,1)} %down_hbm.1), custom_call_target="tpu_custom_call" | custom-call | flops 1509949440 | bytes 16777216 | tf_op jit(solution)/shard_map/moe_input_grad/pallas_call | solution.py:310
  95.6 1.5 %copy.9 = bf16[16,2048]{1,0:T(8,128)(2,1)} copy(bf16[16,2048]{1,0:T(8,128)(2,1)} %moe_input_grad.1) | data formatting | bytes 131072

commit v3 on v2

--- a/solution.py
+++ b/solution.py
@@ -13,14 +13,16 @@
 
 ROWS = 24
 SLOT = 32
-DC = 512
+DC = 1024
+HC = DC // 2
+LAGS = (0, 1, 2, 3)
 
 
 def body(
     nz, nx, ny,
     tok_hbm, routes_hbm, gates_hbm, grad_hbm, gate_hbm, up_hbm, down_hbm,
     out_ref,
-    wbuf, tok, grd, rts, gts, xs, xr, lhs, acc, hid, ret_out, ret_in, part, yr,
+    wbuf, tok, grd, rts, gts, xs, xr, lhs, acc, hid, ret_out, ret_in, part, y_one, y_side, y_sum, yr,
     in_sem, own_sem, z_send, z_recv, p_send, p_recv, x_sem, r_send, r_recv, y_send, y_recv,
 ):
     half = nz // 2
@@ -214,12 +216,16 @@
         for m in range(3):
             forward(p, m)
     service(half)
-    for m in range(3):
-        forward(0, m)
-    gate_pre, up_pre, hidden = acc[0], acc[1], acc[2]
+    forward(0, 0)
+    forward(0, 1)
+    gate_pre, up_pre = acc[0], acc[1]
     sigma = 1.0 / (1.0 + jnp.exp(-gate_pre))
-    hid[0] = (hidden * up_pre * sigma * (1.0 + gate_pre * (1.0 - sigma))).astype(BF16)
-    hid[1] = (hidden * gate_pre * sigma).astype(BF16)
+    acc[0] = up_pre * sigma * (1.0 + gate_pre * (1.0 - sigma))
+    acc[1] = gate_pre * sigma
+    forward(0, 2)
+    hidden = acc[2]
+    hid[0] = (hidden * acc[0]).astype(BF16)
+    hid[1] = (hidden * acc[1]).astype(BF16)
 
     over = (((1,), (1,)), ((), ()))
 
@@ -231,67 +237,94 @@
             term = part_sum if term is None else term + part_sum
         return term
 
-    ret = []
-    for dc in range(n_dc):
-        a, b = backward(2 * dc), backward(2 * dc + 1)
+    def r_copy(dc, r):
+        return pltpu.make_async_remote_copy(
+            src_ref=ret_out.at[dc, r - 1],
+            dst_ref=ret_in.at[dc, r],
+            send_sem=r_send.at[dc, r],
+            recv_sem=r_recv.at[dc, r],
+            device_id=x_back[r],
+            device_id_type=MESH,
+        )
+
+    def send_back(dc):
+        a = [backward(dc * (DC // 256) + i) for i in range(DC // 256)]
+        a = a[0] if len(a) == 1 else jnp.concatenate(a, axis=1)
         for r in range(nx):
             o, q = r * 16, nx * 16 + r * 8
             dest = ret_in.at[dc, 0] if r == 0 else ret_out.at[dc, r - 1]
-            dest[0:16, :] = a[o : o + 16].astype(BF16)
-            dest[16:32, :] = b[o : o + 16].astype(BF16)
-            dest[32:48, :] = jnp.concatenate([a[q : q + 8], b[q : q + 8]], axis=0).astype(BF16)
-        ret.append([])
+            dest[0:16, :] = a[o : o + 16, 0:HC].astype(BF16)
+            dest[16:32, :] = a[o : o + 16, HC:DC].astype(BF16)
+            dest[32:48, :] = jnp.concatenate(
+                [a[q : q + 8, 0:HC], a[q : q + 8, HC:DC]], axis=0
+            ).astype(BF16)
+            if r:
+                start(r_copy(dc, r))
+
+    def rows_of(step):
+        return pl.ds(pl.multiple_of(lax.rem(y + step, ny) * 16, 16), 16)
+
+    def y_copy(dc, i):
+        src, dst, step = (
+            lambda: (part.at[dc, rows_of(ny - 3), :], y_one.at[dc, 0], ny - 1),
+            lambda: (part.at[dc, rows_of(3), :], y_one.at[dc, 1], 1),
+            lambda: (part.at[dc, rows_of(4), pl.ds(0, HC)], y_side.at[dc, 0], ny - 2),
+            lambda: (part.at[dc, rows_of(4), pl.ds(HC, HC)], y_side.at[dc, 1], 2),
+            lambda: (part.at[dc, rows_of(ny - 1), :], yr.at[dc, 0], ny - 1),
+            lambda: (part.at[dc, rows_of(1), :], yr.at[dc, 1], 1),
+            lambda: (y_sum.at[dc, 0], yr.at[dc, 2], ny - 2),
+            lambda: (y_sum.at[dc, 1], yr.at[dc, 3], 2),
+        )[i]()
+        return pltpu.make_async_remote_copy(
+            src_ref=src,
+            dst_ref=dst,
+            send_sem=y_send.at[dc, i],
+            recv_sem=y_recv.at[dc, i],
+            device_id=y_to[step],
+            device_id_type=MESH,
+        )
+
+    def add_groups(dc):
         for r in range(1, nx):
-            copy = pltpu.make_async_remote_copy(
-                src_ref=ret_out.at[dc, r - 1],
-                dst_ref=ret_in.at[dc, r],
-                send_sem=r_send.at[dc, r],
-                recv_sem=r_recv.at[dc, r],
-                device_id=x_back[r],
-                device_id_type=MESH,
-            )
-            start(copy)
-            ret[-1].append(copy)
-    y_copies = []
-    for dc in range(n_dc):
-        for copy in ret[dc]:
-            copy.wait_recv()
+            r_copy(dc, r).wait_recv()
         for h in range(2):
             rows = []
             for r in range(nx):
                 rows += [ret_in[dc, r, h * 16 : h * 16 + 16, :], ret_in[dc, r, 32:48, :]]
-            part[dc, :, h * 256 : h * 256 + 256] = jnp.dot(
+            part[dc, :, h * HC : h * HC + HC] = jnp.dot(
                 spread[h], jnp.concatenate(rows, axis=0), preferred_element_type=F32
             ).astype(BF16)
-        y_copies.append([])
-        for i in range(1, ny):
-            to = pl.multiple_of(lax.rem(y + i, ny) * 16, 16)
-            copy = pltpu.make_async_remote_copy(
-                src_ref=part.at[dc, pl.ds(to, 16), :],
-                dst_ref=yr.at[dc, i - 1],
-                send_sem=y_send.at[dc, i],
-                recv_sem=y_recv.at[dc, i],
-                device_id=y_to[i],
-                device_id_type=MESH,
-            )
-            start(copy)
-            y_copies[-1].append(copy)
-    for dc in range(n_dc):
-        total = part[dc, pl.ds(pl.multiple_of(y * 16, 16), 16), :].astype(F32)
-        for i in range(1, ny):
-            y_copies[dc][i - 1].wait_recv()
-            total += yr[dc, i - 1].astype(F32)
+        for i in range(6):
+            start(y_copy(dc, i))
+
+    def pass_on(dc):
+        for side, step in enumerate((ny - 2, 2)):
+            y_copy(dc, side).wait_recv()
+            y_copy(dc, 2 + side).wait_recv()
+            total = part[dc, rows_of(step), :].astype(F32) + y_one[dc, side].astype(F32)
+            cols = slice(side * HC, side * HC + HC)
+            far = total[:, cols] + y_side[dc, side].astype(F32)
+            near = total[:, HC - side * HC : DC - side * HC]
+            y_sum[dc, side, :, cols] = far.astype(BF16)
+            y_sum[dc, side, :, HC - side * HC : DC - side * HC] = near.astype(BF16)
+            start(y_copy(dc, 6 + side))
+
+    def finish(dc):
+        total = part[dc, rows_of(0), :].astype(F32)
+        for i in range(4):
+            y_copy(dc, 4 + i).wait_recv()
+            total += yr[dc, i].astype(F32)
         total = total.astype(BF16)
         for i in range(DC // 128):
-            pos = dc * (DC // 128) + i
-            p = pos // 2
-            if pos % 2 == 0:
-                src = lax.rem(z + nz - p, nz)
-            else:
-                src = lax.rem(z + (half if p == 0 else p), nz)
-            out_ref[:, pl.ds(pl.multiple_of(src * 128, 128), 128)] = total[
-                :, i * 128 : i * 128 + 128
-            ]
+            p = (dc * (DC // 128) + i) // 2
+            src = z + (half if p == 0 else p) if i % 2 else z + nz - p
+            cols = pl.ds(pl.multiple_of(lax.rem(src, nz) * 128, 128), 128)
+            out_ref[:, cols] = total[:, i * 128 : i * 128 + 128]
+
+    for t in range(n_dc + LAGS[3]):
+        for stage, lag in zip((send_back, add_groups, pass_on, finish), LAGS):
+            if 0 <= t - lag < n_dc:
+                stage(t - lag)
     for copy in sent:
         copy.wait_send()
 
@@ -323,10 +356,13 @@
                 pltpu.VMEM((2, rows, width), BF16),
                 pltpu.VMEM((3, rows, units), F32),
                 pltpu.VMEM((2, rows, units), BF16),
-                pltpu.VMEM((n_dc, nx - 1, 48, 256), BF16),
-                pltpu.VMEM((n_dc, nx, 48, 256), BF16),
+                pltpu.VMEM((n_dc, nx - 1, 48, HC), BF16),
+                pltpu.VMEM((n_dc, nx, 48, HC), BF16),
                 pltpu.VMEM((n_dc, n_tok, DC), BF16),
-                pltpu.VMEM((n_dc, max(ny - 1, 1), n_tok // ny, DC), BF16),
+                pltpu.VMEM((n_dc, 2, n_tok // ny, DC), BF16),
+                pltpu.VMEM((n_dc, 2, n_tok // ny, HC), BF16),
+                pltpu.VMEM((n_dc, 2, n_tok // ny, DC), BF16),
+                pltpu.VMEM((n_dc, 4, n_tok // ny, DC), BF16),
                 dma((4,)),
                 dma((3,)),
                 dma((half + 1, 3, 2)),
@@ -336,8 +372,8 @@
                 dma((2, nx)),
                 dma((n_dc, nx)),
                 dma((n_dc, nx)),
-                dma((n_dc, ny)),
-                dma((n_dc, ny)),
+                dma((n_dc, 8)),
+                dma((n_dc, 8)),
             ],
             compiler_params=pltpu.CompilerParams(
                 collective_id=0, has_side_effects=True, vmem_limit_bytes=60 * 1024 * 1024

time: 97.2 us -> 94.4 us (0.971)
  Pallas kernels: 95.6 us -> 92.8 us
    pallas_call x1, Pallas kernels: 95.6 us -> 92.8 us  [local(): pl.pallas_call(functools.partial(body, nz, nx, ny), out_shape=jax.ShapeDt...]
where the time goes in v3:
time: 94.4 us; the launch traced here: 94.2 us
  Pallas kernels  92.8 us (98%)
  local copies, waits for them, and re-layouts  1.47 us (2%)
    pallas_call x1, Pallas kernels, local(): pl.pallas_call(functools.partial(body, nz, nx, ny), out_shape=jax.ShapeDt...  92.8 us

profile of v3, /device:TPU:1, one launch (start us, length us, event | category | flops | bytes accessed | tf_op | source)
XLA Modules:
  0.0 94.2 jit_solution(11168301390611377555)
XLA Ops:
  0.0 92.8 %moe_input_grad.1 = bf16[16,2048]{1,0:T(8,128)(2,1)} custom-call(bf16[128,2048]{1,0:T(8,128)(2,1)} %tok_hbm.1, s32[6,128]{1,0:T(8,128)} %bitcast.2, f32[6,128]{1,0:T(8,128)} %bitcast.3, bf16[128,2048]{1,0:T(8,128)(2,1)} %grad_hbm.1, bf16[1,64,768]{2,1,0:T(8,128)(2,1)} %gate_hbm.1, bf16[1,64,768]{2,1,0:T(8,128)(2,1)} %up_hbm.1, bf16[1,64,768]{2,1,0:T(8,128)(2,1)} %down_hbm.1), custom_call_target="tpu_custom_call" | custom-call | flops 1509949440 | bytes 16777216 | tf_op jit(solution)/shard_map/moe_input_grad/pallas_call | solution.py:343
  92.8 1.5 %copy.9 = bf16[16,2048]{1,0:T(8,128)(2,1)} copy(bf16[16,2048]{1,0:T(8,128)(2,1)} %moe_input_grad.1) | data formatting | bytes 131072

commit v4 on v2

--- a/solution.py
+++ b/solution.py
@@ -13,19 +13,19 @@
 
 ROWS = 24
 SLOT = 32
-DC = 512
+NEAR = (0, -1, 1, 2, -2)
+QUADS = 4
 
 
 def body(
     nz, nx, ny,
     tok_hbm, routes_hbm, gates_hbm, grad_hbm, gate_hbm, up_hbm, down_hbm,
     out_ref,
-    wbuf, tok, grd, rts, gts, xs, xr, lhs, acc, hid, ret_out, ret_in, part, yr,
-    in_sem, own_sem, z_send, z_recv, p_send, p_recv, x_sem, r_send, r_recv, y_send, y_recv,
+    wbuf, tok, grd, rts, gts, xs, xr, lhs, acc, hid, spread, near_out, near_in, far_out, far_in, part, fin,
+    in_sem, own_sem, z_send, z_recv, p_send, p_recv, x_sem, n_send, n_recv, f_send, f_recv, y_send, y_recv,
 ):
     half = nz // 2
     pairs = nz // 2
-    n_dc = nz * 128 // DC
     dp = lax.axis_index("dp")
     x = lax.axis_index("node")
     y = lax.axis_index("innode")
@@ -35,8 +35,11 @@
     ring = ({"dp": nxt}, {"dp": prv})
     partner = {"dp": z * 2 + 1 - c}
     x_to = [{"node": lax.rem(x + r, nx)} for r in range(nx)]
-    x_back = [{"node": lax.rem(x + nx - r, nx)} for r in range(nx)]
-    y_to = [{"innode": lax.rem(y + i, ny)} for i in range(ny)]
+    y_at = [lax.rem(y + i, ny) for i in range(ny)]
+
+    def back_to(r, step):
+        return {"node": lax.rem(x + nx - r, nx), "innode": y_at[step % ny]}
+
 
     def mine(m, pos, count):
         return wbuf.at[m, pl.ds(pos, count), pl.ds(pl.multiple_of(c * 64, 64), 64), :]
@@ -60,7 +63,9 @@
         ins.append(copy)
 
     barrier = pltpu.get_barrier_semaphore()
-    peers = [ring[0], ring[1], partner] + x_to[1:] + y_to[1:]
+    peers = [ring[0], ring[1], partner]
+    peers += [back_to(r, i) for r in range(nx) for i in (-2, -1, 0, 1, 2) if r or i]
+    peers += [back_to(0, i) for i in range(3, ny - 2)]
     for peer in peers:
         pl.semaphore_signal(barrier, inc=1, device_id=peer, device_id_type=MESH)
     pl.semaphore_wait(barrier, len(peers))
@@ -116,26 +121,34 @@
     lanes = nx * SLOT
     line = lax.broadcasted_iota(jnp.int32, (lanes, n_tok), 0)
     slot = line & (SLOT - 1)
+    slot1 = jnp.where(slot < 16, slot, jnp.where(slot >= 24, slot - 8, -1))
     group = x + (line >> 5)
     group = jnp.where(group >= nx, group - nx, group)
-    expert = group * ny + y
-    hit = jnp.zeros((lanes, n_tok), F32)
-    weight = jnp.zeros((lanes, n_tok), F32)
-    for k in range(rts.shape[0]):
-        same = rts[k : k + 1, :] == expert
-        hit = jnp.where(same, 1.0, hit)
-        weight = jnp.where(same, gts[k : k + 1, :], weight)
     earlier = (
         lax.broadcasted_iota(jnp.int32, (n_tok, n_tok), 0)
         < lax.broadcasted_iota(jnp.int32, (n_tok, n_tok), 1)
     ).astype(F32).astype(BF16)
-    rank = jnp.dot(hit.astype(BF16), earlier, preferred_element_type=F32)
-    slot1 = jnp.where(slot < 16, slot, jnp.where(slot >= 24, slot - 8, -1))
-    own0 = jnp.where(rank == slot.astype(F32), hit, 0.0)
-    own1 = jnp.where(rank == slot1.astype(F32), hit, 0.0)
-    pick = own0.astype(BF16)
-    scale = jnp.sum(own0 * weight, axis=1, keepdims=True)
-    spread = (jnp.transpose(own0).astype(BF16), jnp.transpose(own1).astype(BF16))
+
+    def find(step):
+        expert = group * ny + y_at[step % ny]
+        hit = jnp.zeros((lanes, n_tok), F32)
+        weight = jnp.zeros((lanes, n_tok), F32)
+        for k in range(rts.shape[0]):
+            same = rts[k : k + 1, :] == expert
+            hit = jnp.where(same, 1.0, hit)
+            weight = jnp.where(same, gts[k : k + 1, :], weight)
+        rank = jnp.dot(hit.astype(BF16), earlier, preferred_element_type=F32)
+        own0 = jnp.where(rank == slot.astype(F32), hit, 0.0)
+        own1 = jnp.where(rank == slot1.astype(F32), hit, 0.0)
+        return own0, own1, weight
+
+    def keep(i, rows):
+        for h in range(2):
+            spread[i, h] = jnp.transpose(rows[h]).astype(BF16)
+
+    own_rows = find(0)
+    pick = own_rows[0].astype(BF16)
+    scale = jnp.sum(own_rows[0] * own_rows[2], axis=1, keepdims=True)
 
     ins[2].wait()
     ins[3].wait()
@@ -167,6 +180,8 @@
         start(copy)
         x_copies.append(copy)
 
+    keep(0, own_rows)
+
     def assemble():
         for copy in x_copies:
             copy.wait_recv()
@@ -209,89 +224,136 @@
                 p = ready.pop(0)
                 for m in range(3):
                     forward(p, m)
+            if s > wait_steps:
+                i = s - wait_steps
+                keep(i, find(NEAR[i]))
         ready.append(s)
     for p in ready:
         for m in range(3):
             forward(p, m)
     service(half)
-    for m in range(3):
-        forward(0, m)
-    gate_pre, up_pre, hidden = acc[0], acc[1], acc[2]
+    forward(0, 0)
+    forward(0, 1)
+    gate_pre, up_pre = acc[0], acc[1]
     sigma = 1.0 / (1.0 + jnp.exp(-gate_pre))
-    hid[0] = (hidden * up_pre * sigma * (1.0 + gate_pre * (1.0 - sigma))).astype(BF16)
-    hid[1] = (hidden * gate_pre * sigma).astype(BF16)
+    acc[0] = up_pre * sigma * (1.0 + gate_pre * (1.0 - sigma))
+    acc[1] = gate_pre * sigma
+    forward(0, 2)
+    hidden = acc[2]
+    hid[0] = (hidden * acc[0]).astype(BF16)
+    hid[1] = (hidden * acc[1]).astype(BF16)
 
     over = (((1,), (1,)), ((), ()))
 
     def backward(p):
         term = None
         for m in range(2):
-            rhs = wbuf[m, 2 * p : 2 * p + 2].reshape(256, wbuf.shape[3])
+            rhs = wbuf[m, pl.ds(2 * p, 2)].reshape(256, wbuf.shape[3])
             part_sum = lax.dot_general(hid[m], rhs, over, preferred_element_type=F32)
             term = part_sum if term is None else term + part_sum
         return term
 
-    ret = []
-    for dc in range(n_dc):
-        a, b = backward(2 * dc), backward(2 * dc + 1)
+    def fold(dest, a, b):
+        def put(r):
+            o, q = r * 16, nx * 16 + r * 8
+            dest(r)[0:16, :] = a[o : o + 16].astype(BF16)
+            dest(r)[16:32, :] = b[o : o + 16].astype(BF16)
+            dest(r)[32:48, :] = jnp.concatenate([a[q : q + 8], b[q : q + 8]], axis=0).astype(BF16)
+
+        return put
+
+    def near_copy(i, r):
+        return pltpu.make_async_remote_copy(
+            src_ref=near_out.at[i, r],
+            dst_ref=near_in.at[i, r],
+            send_sem=n_send.at[i, r],
+            recv_sem=n_recv.at[i, r],
+            device_id=back_to(r, -NEAR[i]),
+            device_id_type=MESH,
+        )
+
+    def far_copy(h, r):
+        return pltpu.make_async_remote_copy(
+            src_ref=far_out.at[h, r],
+            dst_ref=far_in.at[h, r],
+            send_sem=f_send.at[h, r],
+            recv_sem=f_recv.at[h, r],
+            device_id=back_to(r, -NEAR[3 + h]),
+            device_id_type=MESH,
+        )
+
+    across = (2, 1, 3, 0)
+    quad = [lax.rem(y + k, QUADS) for k in range(QUADS)]
+    for h in range(2):
+        a = backward(2 * quad[2] + h)
+        put = fold(lambda r: far_out.at[h, r], a[:, :128], a[:, 128:])
+        for r in across:
+            put(r)
+            start(far_copy(h, r))
+    for i, k in ((1, 1), (2, 3), (0, 0)):
+        a, b = backward(2 * quad[k]), backward(2 * quad[k] + 1)
+        put = fold(lambda r: near_out.at[i, r] if r or i else near_in.at[0, 0], a, b)
+        for r in across:
+            put(r)
+            if r or i:
+                start(near_copy(i, r))
+
+    for i in (0, 1, 2):
         for r in range(nx):
-            o, q = r * 16, nx * 16 + r * 8
-            dest = ret_in.at[dc, 0] if r == 0 else ret_out.at[dc, r - 1]
-            dest[0:16, :] = a[o : o + 16].astype(BF16)
-            dest[16:32, :] = b[o : o + 16].astype(BF16)
-            dest[32:48, :] = jnp.concatenate([a[q : q + 8], b[q : q + 8]], axis=0).astype(BF16)
-        ret.append([])
-        for r in range(1, nx):
-            copy = pltpu.make_async_remote_copy(
-                src_ref=ret_out.at[dc, r - 1],
-                dst_ref=ret_in.at[dc, r],
-                send_sem=r_send.at[dc, r],
-                recv_sem=r_recv.at[dc, r],
-                device_id=x_back[r],
-                device_id_type=MESH,
-            )
-            start(copy)
-            ret[-1].append(copy)
-    y_copies = []
-    for dc in range(n_dc):
-        for copy in ret[dc]:
-            copy.wait_recv()
-        for h in range(2):
+            if r or i:
+                near_copy(i, r).wait_recv()
+    for h in range(2):
+        for r in range(nx):
+            far_copy(h, r).wait_recv()
+        total = None
+        for i in (0, 1, 2):
             rows = []
             for r in range(nx):
-                rows += [ret_in[dc, r, h * 16 : h * 16 + 16, :], ret_in[dc, r, 32:48, :]]
-            part[dc, :, h * 256 : h * 256 + 256] = jnp.dot(
-                spread[h], jnp.concatenate(rows, axis=0), preferred_element_type=F32
-            ).astype(BF16)
-        y_copies.append([])
-        for i in range(1, ny):
-            to = pl.multiple_of(lax.rem(y + i, ny) * 16, 16)
-            copy = pltpu.make_async_remote_copy(
-                src_ref=part.at[dc, pl.ds(to, 16), :],
-                dst_ref=yr.at[dc, i - 1],
-                send_sem=y_send.at[dc, i],
-                recv_sem=y_recv.at[dc, i],
-                device_id=y_to[i],
-                device_id_type=MESH,
+                rows += [near_in[i, r, h * 16 : h * 16 + 16, :], near_in[i, r, 32:48, :]]
+            term = jnp.dot(
+                spread[i, h], jnp.concatenate(rows, axis=0), preferred_element_type=F32
             )
-            start(copy)
-            y_copies[-1].append(copy)
-    for dc in range(n_dc):
-        total = part[dc, pl.ds(pl.multiple_of(y * 16, 16), 16), :].astype(F32)
-        for i in range(1, ny):
-            y_copies[dc][i - 1].wait_recv()
-            total += yr[dc, i - 1].astype(F32)
-        total = total.astype(BF16)
-        for i in range(DC // 128):
-            pos = dc * (DC // 128) + i
-            p = pos // 2
-            if pos % 2 == 0:
-                src = lax.rem(z + nz - p, nz)
-            else:
-                src = lax.rem(z + (half if p == 0 else p), nz)
-            out_ref[:, pl.ds(pl.multiple_of(src * 128, 128), 128)] = total[
-                :, i * 128 : i * 128 + 128
+            total = term if total is None else total + term
+        rows = []
+        for r in range(nx):
+            rest = far_in[h, r, 32:48, :].astype(F32)
+            rest = jnp.concatenate([rest[0:8], rest[8:16]], axis=1)
+            rows += [
+                jnp.concatenate([far_in[h, r, 0:16, :], far_in[h, r, 16:32, :]], axis=1),
+                jnp.concatenate([rest, jnp.zeros_like(rest)], axis=0).astype(BF16),
             ]
+        total += jnp.dot(
+            spread[3 + h, 0], jnp.concatenate(rows, axis=0), preferred_element_type=F32
+        )
+        part[h] = total.astype(BF16)
+
+    def rows_of(i):
+        return pl.ds(pl.multiple_of(y_at[i] * 16, 16), 16)
+
+    def y_copy(i):
+        return pltpu.make_async_remote_copy(
+            src_ref=part.at[:, rows_of(i), :],
+            dst_ref=fin.at[i - 1],
+            send_sem=y_send.at[i],
+            recv_sem=y_recv.at[i],
+            device_id=back_to(0, i),
+            device_id_type=MESH,
+        )
+
+    for i in (4, 3, 5, 2, 6, 1, 7):
+        start(y_copy(i))
+    for i in (1, 2, 3, 0):
+        if i:
+            y_copy(i).wait_recv()
+        y_copy(i + 4).wait_recv()
+        q = lax.rem(y + ny - i, QUADS)
+        for h in range(2):
+            mine_too = fin[i - 1, h] if i else part[h, rows_of(0), :]
+            total = (mine_too.astype(F32) + fin[i + 3, h].astype(F32)).astype(BF16)
+            p = 2 * q + h
+            for side, src in enumerate((z + nz - p, z + jnp.where(p == 0, half, p))):
+                cols = pl.ds(pl.multiple_of(lax.rem(src, nz) * 128, 128), 128)
+                out_ref[:, cols] = total[:, side * 128 : side * 128 + 128]
     for copy in sent:
         copy.wait_send()
 
@@ -303,7 +365,7 @@
         n_tok, width = tokens.shape
         units = gate_weight.shape[2]
         rows = nx * ROWS
-        n_dc = width // DC
+        assert (nx, ny, nz, width, n_tok) == (4, 8, 16, 2048, 128)
         half = nz // 2
         any_space = pl.BlockSpec(memory_space=pl.ANY)
         dma = pltpu.SemaphoreType.DMA
@@ -323,10 +385,13 @@
                 pltpu.VMEM((2, rows, width), BF16),
                 pltpu.VMEM((3, rows, units), F32),
                 pltpu.VMEM((2, rows, units), BF16),
-                pltpu.VMEM((n_dc, nx - 1, 48, 256), BF16),
-                pltpu.VMEM((n_dc, nx, 48, 256), BF16),
-                pltpu.VMEM((n_dc, n_tok, DC), BF16),
-                pltpu.VMEM((n_dc, max(ny - 1, 1), n_tok // ny, DC), BF16),
+                pltpu.VMEM((5, 2, n_tok, nx * SLOT), BF16),
+                pltpu.VMEM((3, nx, 48, 256), BF16),
+                pltpu.VMEM((3, nx, 48, 256), BF16),
+                pltpu.VMEM((2, nx, 48, 128), BF16),
+                pltpu.VMEM((2, nx, 48, 128), BF16),
+                pltpu.VMEM((2, n_tok, 256), BF16),
+                pltpu.VMEM((ny - 1, 2, n_tok // ny, 256), BF16),
                 dma((4,)),
                 dma((3,)),
                 dma((half + 1, 3, 2)),
@@ -334,10 +399,12 @@
                 dma((half + 1, 3)),
                 dma((half + 1, 3)),
                 dma((2, nx)),
-                dma((n_dc, nx)),
-                dma((n_dc, nx)),
-                dma((n_dc, ny)),
-                dma((n_dc, ny)),
+                dma((3, nx)),
+                dma((3, nx)),
+                dma((2, nx)),
+                dma((2, nx)),
+                dma((ny,)),
+                dma((ny,)),
             ],
             compiler_params=pltpu.CompilerParams(
                 collective_id=0, has_side_effects=True, vmem_limit_bytes=60 * 1024 * 1024

time: 97.2 us -> 93.2 us (0.959)
  Pallas kernels: 95.6 us -> 91.5 us
    pallas_call x1, Pallas kernels: 95.6 us -> 91.5 us  [local(): pl.pallas_call(functools.partial(body, nz, nx, ny), out_shape=jax.ShapeDt...]
where the time goes in v4:
time: 93.2 us; the launch traced here: 93 us
  Pallas kernels  91.5 us (98%)
  local copies, waits for them, and re-layouts  1.47 us (2%)
    pallas_call x1, Pallas kernels, local(): pl.pallas_call(functools.partial(body, nz, nx, ny), out_shape=jax.ShapeDt...  91.5 us

profile of v4, /device:TPU:1, one launch (start us, length us, event | category | flops | bytes accessed | tf_op | source)
XLA Modules:
  0.0 93.0 jit_solution(5996629715775212301)
XLA Ops:
  0.0 91.5 %moe_input_grad.1 = bf16[16,2048]{1,0:T(8,128)(2,1)} custom-call(bf16[128,2048]{1,0:T(8,128)(2,1)} %tok_hbm.1, s32[6,128]{1,0:T(8,128)} %bitcast.2, f32[6,128]{1,0:T(8,128)} %bitcast.3, bf16[128,2048]{1,0:T(8,128)(2,1)} %grad_hbm.1, bf16[1,64,768]{2,1,0:T(8,128)(2,1)} %gate_hbm.1, bf16[1,64,768]{2,1,0:T(8,128)(2,1)} %up_hbm.1, bf16[1,64,768]{2,1,0:T(8,128)(2,1)} %down_hbm.1), custom_call_target="tpu_custom_call" | custom-call | flops 1509949440 | bytes 16777216 | tf_op jit(solution)/shard_map/moe_input_grad/pallas_call | solution.py:372
  91.5 1.5 %copy.9 = bf16[16,2048]{1,0:T(8,128)(2,1)} copy(bf16[16,2048]{1,0:T(8,128)(2,1)} %moe_input_grad.1) | data formatting | bytes 131072

commit v5 on v4

--- a/solution.py
+++ b/solution.py
@@ -21,8 +21,8 @@
     nz, nx, ny,
     tok_hbm, routes_hbm, gates_hbm, grad_hbm, gate_hbm, up_hbm, down_hbm,
     out_ref,
-    wbuf, tok, grd, rts, gts, xs, xr, lhs, acc, hid, spread, near_out, near_in, far_out, far_in, part, fin,
-    in_sem, own_sem, z_send, z_recv, p_send, p_recv, x_sem, n_send, n_recv, f_send, f_recv, y_send, y_recv,
+    wbuf, tok, grd, rts, gts, xs, xr, lhs, acc, hid, spread, near_out, near_in, far_out, far_in, part,
+    in_sem, own_sem, z_send, z_recv, e_send, e_recv, p_send, p_recv, x_sem, n_send, n_recv, f_send, f_recv, y_send, y_recv,
 ):
     half = nz // 2
     pairs = nz // 2
@@ -34,6 +34,7 @@
     prv = lax.rem(z + nz - 1, nz) * 2 + c
     ring = ({"dp": nxt}, {"dp": prv})
     partner = {"dp": z * 2 + 1 - c}
+    cross = ({"dp": nxt + 1 - 2 * c}, {"dp": prv + 1 - 2 * c})
     x_to = [{"node": lax.rem(x + r, nx)} for r in range(nx)]
     y_at = [lax.rem(y + i, ny) for i in range(ny)]
 
@@ -63,7 +64,7 @@
         ins.append(copy)
 
     barrier = pltpu.get_barrier_semaphore()
-    peers = [ring[0], ring[1], partner]
+    peers = [ring[0], ring[1], partner, cross[0], cross[1]]
     peers += [back_to(r, i) for r in range(nx) for i in (-2, -1, 0, 1, 2) if r or i]
     peers += [back_to(0, i) for i in range(3, ny - 2)]
     for peer in peers:
@@ -77,6 +78,16 @@
             send_sem=z_send.at[s, m, d],
             recv_sem=z_recv.at[s, m, d],
             device_id=ring[d],
+            device_id_type=MESH,
+        )
+
+    def e_copy(d):
+        return pltpu.make_async_remote_copy(
+            src_ref=piece(2, place(half - 1, d), half, d),
+            dst_ref=piece(2, place(half, d), half, d),
+            send_sem=e_send.at[d],
+            recv_sem=e_recv.at[d],
+            device_id=cross[d],
             device_id_type=MESH,
         )
 
@@ -106,7 +117,10 @@
                 z_copy(s, m, d).wait_recv()
                 if s < half:
                     start(z_copy(s + 1, m, d))
-            start(p_copy(s, m))
+                if s + 1 == half and m == 2:
+                    start(e_copy(d))
+            if s < half or m < 2:
+                start(p_copy(s, m))
 
     for m in range(3):
         own[m].wait()
@@ -196,22 +210,30 @@
             lhs[0, o : o + 16, :] = jnp.concatenate([a[0:8], b[0:8]], axis=0).astype(BF16)
             lhs[1, o : o + 16, :] = jnp.concatenate([a[8:16], b[8:16]], axis=0).astype(BF16)
 
-    def forward(p, m):
-        if p == 0:
-            p_copy(0, m).wait_recv()
-            p_copy(half, m).wait_recv()
-        else:
-            p_copy(p, m).wait_recv()
-        width = wbuf.shape[3]
+    def add(m, pos, count, fresh=False):
         term = jnp.dot(
-            lhs[m // 2, :, p * 256 : p * 256 + 256],
-            wbuf[m, 2 * p : 2 * p + 2].reshape(256, width),
+            lhs[m // 2, :, pos * 128 : (pos + count) * 128],
+            wbuf[m, pos : pos + count].reshape(count * 128, wbuf.shape[3]),
             preferred_element_type=F32,
         )
-        if p == (1 if pairs > 1 else 0):
+        if fresh:
             acc[m] = term
         else:
             acc[m] += term
+
+    def forward(p, m):
+        p_copy(p, m).wait_recv()
+        add(m, 2 * p, 2, p == 1)
+
+    def forward_last(m):
+        if m < 2:
+            p_copy(half, m).wait_recv()
+            p_copy(0, m).wait_recv()
+            add(m, 0, 2)
+        else:
+            e_copy(0).wait_recv()
+            e_copy(1).wait_recv()
+            add(m, 1, 1)
 
     wait_steps = min(3, half - 1)
     ready = []
@@ -231,24 +253,32 @@
     for p in ready:
         for m in range(3):
             forward(p, m)
+    p_copy(0, 2).wait_recv()
+    add(2, 0, 1)
     service(half)
-    forward(0, 0)
-    forward(0, 1)
+    forward_last(0)
+    forward_last(1)
     gate_pre, up_pre = acc[0], acc[1]
     sigma = 1.0 / (1.0 + jnp.exp(-gate_pre))
     acc[0] = up_pre * sigma * (1.0 + gate_pre * (1.0 - sigma))
     acc[1] = gate_pre * sigma
-    forward(0, 2)
+    forward_last(2)
     hidden = acc[2]
     hid[0] = (hidden * acc[0]).astype(BF16)
     hid[1] = (hidden * acc[1]).astype(BF16)
 
     over = (((1,), (1,)), ((), ()))
 
+    def held(block):
+        away = lax.rem(z + nz - block, nz)
+        low = jnp.where(away == 0, 0, 2 * away)
+        return jnp.where(away < half, low, jnp.where(away == half, 1, 2 * (nz - away) + 1))
+
     def backward(p):
         term = None
+        first, second = held(2 * p), held(2 * p + 1)
         for m in range(2):
-            rhs = wbuf[m, pl.ds(2 * p, 2)].reshape(256, wbuf.shape[3])
+            rhs = jnp.concatenate([wbuf[m, first], wbuf[m, second]], axis=0)
             part_sum = lax.dot_general(hid[m], rhs, over, preferred_element_type=F32)
             term = part_sum if term is None else term + part_sum
         return term
@@ -298,42 +328,47 @@
             if r or i:
                 start(near_copy(i, r))
 
-    for i in (0, 1, 2):
-        for r in range(nx):
-            if r or i:
-                near_copy(i, r).wait_recv()
+    sums = []
     for h in range(2):
+        rows = []
         for r in range(nx):
             far_copy(h, r).wait_recv()
-        total = None
-        for i in (0, 1, 2):
-            rows = []
-            for r in range(nx):
-                rows += [near_in[i, r, h * 16 : h * 16 + 16, :], near_in[i, r, 32:48, :]]
-            term = jnp.dot(
-                spread[i, h], jnp.concatenate(rows, axis=0), preferred_element_type=F32
-            )
-            total = term if total is None else total + term
-        rows = []
-        for r in range(nx):
             rest = far_in[h, r, 32:48, :].astype(F32)
             rest = jnp.concatenate([rest[0:8], rest[8:16]], axis=1)
             rows += [
                 jnp.concatenate([far_in[h, r, 0:16, :], far_in[h, r, 16:32, :]], axis=1),
                 jnp.concatenate([rest, jnp.zeros_like(rest)], axis=0).astype(BF16),
             ]
-        total += jnp.dot(
-            spread[3 + h, 0], jnp.concatenate(rows, axis=0), preferred_element_type=F32
-        )
-        part[h] = total.astype(BF16)
+        sums.append(
+            jnp.dot(
+                spread[3 + h, 0], jnp.concatenate(rows, axis=0), preferred_element_type=F32
+            )
+        )
+    for i in (1, 2, 0):
+        for r in range(nx):
+            if r or i:
+                near_copy(i, r).wait_recv()
+        for h in range(2):
+            rows = []
+            for r in range(nx):
+                rows += [near_in[i, r, h * 16 : h * 16 + 16, :], near_in[i, r, 32:48, :]]
+            sums[h] += jnp.dot(
+                spread[i, h], jnp.concatenate(rows, axis=0), preferred_element_type=F32
+            )
+    for h in range(2):
+        part[:, h * 256 : h * 256 + 256] = sums[h].astype(BF16)
 
     def rows_of(i):
         return pl.ds(pl.multiple_of(y_at[i] * 16, 16), 16)
 
+    place_out = out_ref.at[
+        lax.div(y, QUADS), :, pl.ds(pl.multiple_of(quad[0] * 512, 512), 512)
+    ]
+
     def y_copy(i):
         return pltpu.make_async_remote_copy(
-            src_ref=part.at[:, rows_of(i), :],
-            dst_ref=fin.at[i - 1],
+            src_ref=part.at[rows_of(i), :],
+            dst_ref=place_out,
             send_sem=y_send.at[i],
             recv_sem=y_recv.at[i],
             device_id=back_to(0, i),
@@ -342,18 +377,11 @@
 
     for i in (4, 3, 5, 2, 6, 1, 7):
         start(y_copy(i))
-    for i in (1, 2, 3, 0):
-        if i:
-            y_copy(i).wait_recv()
-        y_copy(i + 4).wait_recv()
-        q = lax.rem(y + ny - i, QUADS)
-        for h in range(2):
-            mine_too = fin[i - 1, h] if i else part[h, rows_of(0), :]
-            total = (mine_too.astype(F32) + fin[i + 3, h].astype(F32)).astype(BF16)
-            p = 2 * q + h
-            for side, src in enumerate((z + nz - p, z + jnp.where(p == 0, half, p))):
-                cols = pl.ds(pl.multiple_of(lax.rem(src, nz) * 128, 128), 128)
-                out_ref[:, cols] = total[:, side * 128 : side * 128 + 128]
+    kept = pltpu.make_async_copy(part.at[rows_of(0), :], place_out, y_send.at[0])
+    kept.start()
+    for i in range(1, ny):
+        y_copy(i).wait_recv()
+    kept.wait()
     for copy in sent:
         copy.wait_send()
 
@@ -369,11 +397,11 @@
         half = nz // 2
         any_space = pl.BlockSpec(memory_space=pl.ANY)
         dma = pltpu.SemaphoreType.DMA
-        return pl.pallas_call(
+        halves = pl.pallas_call(
             functools.partial(body, nz, nx, ny),
-            out_shape=jax.ShapeDtypeStruct((n_tok // ny, width), BF16),
+            out_shape=jax.ShapeDtypeStruct((2, n_tok // ny, width), BF16),
             in_specs=[any_space] * 7,
-            out_specs=pl.BlockSpec(memory_space=pltpu.VMEM),
+            out_specs=any_space,
             scratch_shapes=[
                 pltpu.VMEM((3, nz, 128, units), BF16),
                 pltpu.VMEM((n_tok, width), BF16),
@@ -390,12 +418,13 @@
                 pltpu.VMEM((3, nx, 48, 256), BF16),
                 pltpu.VMEM((2, nx, 48, 128), BF16),
                 pltpu.VMEM((2, nx, 48, 128), BF16),
-                pltpu.VMEM((2, n_tok, 256), BF16),
-                pltpu.VMEM((ny - 1, 2, n_tok // ny, 256), BF16),
+                pltpu.VMEM((n_tok, 512), BF16),
                 dma((4,)),
                 dma((3,)),
                 dma((half + 1, 3, 2)),
                 dma((half + 1, 3, 2)),
+                dma((2,)),
+                dma((2,)),
                 dma((half + 1, 3)),
                 dma((half + 1, 3)),
                 dma((2, nx)),
@@ -416,6 +445,7 @@
             ),
             name="moe_input_grad",
         )(tokens, routes.T, route_gates.T, out_grad, gate_weight, up_weight, down_weight)
+        return (halves[0].astype(F32) + halves[1].astype(F32)).astype(BF16)
 
     return jax.shard_map(
         local,

time: 93.2 us -> 92.2 us (0.989)
  other arithmetic: 0 us -> 1.52 us
  local copies, waits for them, and re-layouts: 1.47 us -> 0 us
  Pallas kernels: 91.5 us -> 90.5 us
    convert_element_type x0 -> x1, other arithmetic: none -> 1.52 us  [local(): return (halves[0].astype(F32) + halves[1].astype(F32)).astype(BF16)]
    unnamed x1 -> x0, local copies, waits for them, and re-layouts: 1.47 us -> none
    pallas_call x1, Pallas kernels: 91.5 us -> 90.5 us  [local(): pl.pallas_call(functools.partial(body, nz, nx, ny), out_shape=jax.ShapeDt...]
where the time goes in v5:
time: 92.2 us; the launch traced here: 92 us
  Pallas kernels  90.5 us (98%)
  other arithmetic  1.52 us (2%)
    pallas_call x1, Pallas kernels, local(): pl.pallas_call(functools.partial(body, nz, nx, ny), out_shape=jax.ShapeDt...  90.5 us

profile of v5, /device:TPU:1, one launch (start us, length us, event | category | flops | bytes accessed | tf_op | source)
XLA Modules:
  0.0 92.0 jit_solution(11893180085703759869)
XLA Ops:
  0.0 90.5 %moe_input_grad.1 = bf16[2,16,2048]{2,1,0:T(8,128)(2,1)} custom-call(bf16[128,2048]{1,0:T(8,128)(2,1)} %tok_hbm.1, s32[6,128]{1,0:T(8,128)} %bitcast.4, f32[6,128]{1,0:T(8,128)} %bitcast.5, bf16[128,2048]{1,0:T(8,128)(2,1)} %grad_hbm.1, bf16[1,64,768]{2,1,0:T(8,128)(2,1)} %gate_hbm.1, bf16[1,64,768]{2,1,0:T(8,128)(2,1)} %up_hbm.1, bf16[1,64,768]{2,1,0:T(8,128)(2,1)} %down_hbm.1), custom_call_target="tpu_custom_call" | custom-call | flops 1509949440 | bytes 16777216 | tf_op jit(solution)/shard_map/moe_input_grad/pallas_call | solution.py:400
  90.5 1.5 %fusion = bf16[16,2048]{1,0:T(8,128)(2,1)} fusion(bf16[2,16,2048]{2,1,0:T(8,128)(2,1)} %moe_input_grad.1), kind=kLoop, calls=%fused_computation.1 | loop fusion | flops 131072 | bytes 196608 | tf_op jit(solution)/shard_map/convert_element_type | solution.py:448

commit v6 on v5

--- a/solution.py
+++ b/solution.py
@@ -320,7 +320,7 @@
         for r in across:
             put(r)
             start(far_copy(h, r))
-    for i, k in ((1, 1), (2, 3), (0, 0)):
+    for i, k in ((0, 0), (1, 1), (2, 3)):
         a, b = backward(2 * quad[k]), backward(2 * quad[k] + 1)
         put = fold(lambda r: near_out.at[i, r] if r or i else near_in.at[0, 0], a, b)
         for r in across:
@@ -344,7 +344,7 @@
                 spread[3 + h, 0], jnp.concatenate(rows, axis=0), preferred_element_type=F32
             )
         )
-    for i in (1, 2, 0):
+    for i in (0, 1, 2):
         for r in range(nx):
             if r or i:
                 near_copy(i, r).wait_recv()

time: 92.2 us -> 91.4 us (level)
  no operation moved by 1% of the time
where the time goes in v6:
time: 91.4 us; the launch traced here: 91.2 us
  Pallas kernels  89.7 us (98%)
  other arithmetic  1.52 us (2%)
    pallas_call x1, Pallas kernels, local(): pl.pallas_call(functools.partial(body, nz, nx, ny), out_shape=jax.ShapeDt...  89.7 us

profile of v6, /device:TPU:1, one launch (start us, length us, event | category | flops | bytes accessed | tf_op | source)
XLA Modules:
  0.0 91.2 jit_solution(6413532953892402327)
XLA Ops:
  0.0 89.7 %moe_input_grad.1 = bf16[2,16,2048]{2,1,0:T(8,128)(2,1)} custom-call(bf16[128,2048]{1,0:T(8,128)(2,1)} %tok_hbm.1, s32[6,128]{1,0:T(8,128)} %bitcast.4, f32[6,128]{1,0:T(8,128)} %bitcast.5, bf16[128,2048]{1,0:T(8,128)(2,1)} %grad_hbm.1, bf16[1,64,768]{2,1,0:T(8,128)(2,1)} %gate_hbm.1, bf16[1,64,768]{2,1,0:T(8,128)(2,1)} %up_hbm.1, bf16[1,64,768]{2,1,0:T(8,128)(2,1)} %down_hbm.1), custom_call_target="tpu_custom_call" | custom-call | flops 1509949440 | bytes 16777216 | tf_op jit(solution)/shard_map/moe_input_grad/pallas_call | solution.py:400
  89.7 1.5 %fusion = bf16[16,2048]{1,0:T(8,128)(2,1)} fusion(bf16[2,16,2048]{2,1,0:T(8,128)(2,1)} %moe_input_grad.1), kind=kLoop, calls=%fused_computation.1 | loop fusion | flops 131072 | bytes 196608 | tf_op jit(solution)/shard_map/convert_element_type | solution.py:448

commit v7 on v6

--- a/solution.py
+++ b/solution.py
@@ -314,19 +314,23 @@
 
     across = (2, 1, 3, 0)
     quad = [lax.rem(y + k, QUADS) for k in range(QUADS)]
+    def send_near(i, k):
+        a, b = backward(2 * quad[k]), backward(2 * quad[k] + 1)
+        put = fold(lambda r: near_out.at[i, r] if r or i else near_in.at[0, 0], a, b)
+        for r in across:
+            put(r)
+            if r or i:
+                start(near_copy(i, r))
+
+    send_near(0, 0)
     for h in range(2):
         a = backward(2 * quad[2] + h)
         put = fold(lambda r: far_out.at[h, r], a[:, :128], a[:, 128:])
         for r in across:
             put(r)
             start(far_copy(h, r))
-    for i, k in ((0, 0), (1, 1), (2, 3)):
-        a, b = backward(2 * quad[k]), backward(2 * quad[k] + 1)
-        put = fold(lambda r: near_out.at[i, r] if r or i else near_in.at[0, 0], a, b)
-        for r in across:
-            put(r)
-            if r or i:
-                start(near_copy(i, r))
+    send_near(1, 1)
+    send_near(2, 3)
 
     sums = []
     for h in range(2):

time: 91.4 us -> 91.9 us (level)
  no operation moved by 1% of the time
where the time goes in v7:
time: 91.9 us; the launch traced here: 91.8 us
  Pallas kernels  90.2 us (98%)
  other arithmetic  1.52 us (2%)
    pallas_call x1, Pallas kernels, local(): pl.pallas_call(functools.partial(body, nz, nx, ny), out_shape=jax.ShapeDt...  90.2 us

profile of v7, /device:TPU:1, one launch (start us, length us, event | category | flops | bytes accessed | tf_op | source)
XLA Modules:
  0.0 91.8 jit_solution(1505043849073278246)
XLA Ops:
  0.0 90.2 %moe_input_grad.1 = bf16[2,16,2048]{2,1,0:T(8,128)(2,1)} custom-call(bf16[128,2048]{1,0:T(8,128)(2,1)} %tok_hbm.1, s32[6,128]{1,0:T(8,128)} %bitcast.4, f32[6,128]{1,0:T(8,128)} %bitcast.5, bf16[128,2048]{1,0:T(8,128)(2,1)} %grad_hbm.1, bf16[1,64,768]{2,1,0:T(8,128)(2,1)} %gate_hbm.1, bf16[1,64,768]{2,1,0:T(8,128)(2,1)} %up_hbm.1, bf16[1,64,768]{2,1,0:T(8,128)(2,1)} %down_hbm.1), custom_call_target="tpu_custom_call" | custom-call | flops 1509949440 | bytes 16777216 | tf_op jit(solution)/shard_map/moe_input_grad/pallas_call | solution.py:404
  90.2 1.5 %fusion = bf16[16,2048]{1,0:T(8,128)(2,1)} fusion(bf16[2,16,2048]{2,1,0:T(8,128)(2,1)} %moe_input_grad.1), kind=kLoop, calls=%fused_computation.1 | loop fusion | flops 131072 | bytes 196608 | tf_op jit(solution)/shard_map/convert_element_type | solution.py:452
